TPU v7x, 32 devices: a whole 2x2x4 slice. The times are simulated.
32 devices in a mesh: gx: 8 (over z, core), gy: 4 (over y, x).
Axes of the slice: x: 2, y: 2, z: 4, core: 2. Of those that a mesh axis runs over, the one named last changes fastest.
Arguments:
- pressure: float32 [2048, 1024], P('gx', 'gy'), may hold values from -6 to 6
- source: float32 [2048, 1024], P('gx', 'gy'), may hold values from -6 to 6
- conductivity: float32 [2048, 1024], P('gx', 'gy'), may hold values from 0.2 to 5
- storage: float32 [2048, 1024], P('gx', 'gy'), may hold values from 0.2 to 1
Outputs:
- pressure_next: float32 [2048, 1024], P('gx', 'gy')
All inputs are finite; a program needn't handle non-finite values.
Results may differ from a plain program's by a relative error of at most 0.0001.
Values sent between devices are 32-bit elements; how exact they have to be, the bound alone decides.
A program may use at most 128 MiB of HBM per device.

v0:
```python
import jax
import jax.numpy as jnp
from jax import lax
from jax.sharding import PartitionSpec as P

LEVELS_SPLIT = 4
LEVELS_MERGED = 2
COARSE_SWEEPS = 8


OMEGA = 0.8


def with_halo(x, sides, width):
    for axis, dim in sides:
        size, length = (lax.axis_size(axis), x.shape[dim])
        up = [(i, (i + 1) % size) for i in range(size - 1)]
        down = [(j, i) for i, j in up]
        last = lax.slice_in_dim(x, length - width, length, axis=dim)
        first = lax.slice_in_dim(x, 0, width, axis=dim)
        before = lax.ppermute(last, axis, up)
        after = lax.ppermute(first, axis, down)
        x = jnp.concatenate([before, x, after], axis=dim)
    return x


def coarsen(grid):
    height, breadth = grid.shape
    return grid.reshape(height // 2, 2, breadth // 2, 2).sum(axis=(1, 3))


def prolong(grid):
    return jnp.repeat(jnp.repeat(grid, 2, axis=0), 2, axis=1)


def padded_block(field, span_x, span_y):
    if span_x == 1 and span_y == 1:
        return with_halo(field, (("gx", 0), ("gy", 1)), 1)
    height, breadth = field.shape
    lower_row = jnp.zeros((1, breadth), field.dtype)
    upper_row = jnp.zeros((1, breadth), field.dtype)
    lower_col = jnp.zeros((height, 1), field.dtype)
    upper_col = jnp.zeros((height, 1), field.dtype)
    corner = jnp.zeros((1, 1), field.dtype)
    middle = jnp.concatenate([lower_col, field, upper_col], axis=1)
    top_row = jnp.concatenate([corner, lower_row, corner], axis=1)
    bottom_row = jnp.concatenate([corner, upper_row, corner], axis=1)
    return jnp.concatenate([top_row, middle, bottom_row], axis=0)


def face_terms(conduct, stored, span_x, span_y):
    padded = padded_block(conduct, span_x, span_y)
    west_face = 0.5 * (conduct + padded[:-2, 1:-1])
    east_face = 0.5 * (conduct + padded[2:, 1:-1])
    south_face = 0.5 * (conduct + padded[1:-1, :-2])
    north_face = 0.5 * (conduct + padded[1:-1, 2:])
    diagonal = stored + west_face + east_face + south_face + north_face
    return (diagonal, west_face, east_face, south_face, north_face, span_x, span_y)


def pre_smooth(section, right_side, start_field):
    if start_field is None:
        field = first_sweep(right_side, section)
    else:
        field = jacobi_sweep(start_field, right_side, section)
    field = jacobi_sweep(field, right_side, section)
    residual = right_side - operate(field, section)
    return (field, residual, right_side)


def post_smooth(section, right_side, field):
    field = jacobi_sweep(field, right_side, section)
    return jacobi_sweep(field, right_side, section)


def operate(field, section):
    diagonal, west_face, east_face, south_face, north_face = section[:5]
    span_x, span_y = (section[5], section[6])
    padded = padded_block(field, span_x, span_y)
    return (
        diagonal * field
        - west_face * padded[:-2, 1:-1]
        - east_face * padded[2:, 1:-1]
        - south_face * padded[1:-1, :-2]
        - north_face * padded[1:-1, 2:]
    )


def jacobi_sweep(field, right_side, section):
    return field + OMEGA * (right_side - operate(field, section)) / section[0]


def first_sweep(right_side, section):
    return OMEGA * right_side / section[0]


def gather_whole(stacked):
    stacked = lax.all_gather(stacked, "gx", axis=1, tiled=True)
    return lax.all_gather(stacked, "gy", axis=2, tiled=True)


def own_block(correction, block_x, block_y):
    part = lax.dynamic_slice_in_dim(correction, lax.axis_index("gx") * block_x, block_x, 0)
    return lax.dynamic_slice_in_dim(part, lax.axis_index("gy") * block_y, block_y, 1)


def cycle(sections, depth, right_side, start_field):
    section = sections[depth]
    if depth == len(sections) - 1:
        field = first_sweep(right_side, section)
        for _ in range(COARSE_SWEEPS - 1):
            field = jacobi_sweep(field, right_side, section)
        return field
    field, residual, side_wide = pre_smooth(section, right_side, start_field)
    coarse_side = coarsen(residual)
    block_x, block_y = coarse_side.shape
    if depth + 1 >= LEVELS_SPLIT:
        if depth + 1 == LEVELS_SPLIT:
            coarse_side = gather_whole(coarse_side[None])[0]
    correction = cycle(sections, depth + 1, coarse_side, None)
    if depth + 1 >= LEVELS_SPLIT:
        if depth + 1 == LEVELS_SPLIT:
            correction = own_block(correction, block_x, block_y)
    field = field + prolong(correction)
    return post_smooth(section, right_side, field)


def per_device(pressure, source, conductivity, storage):
    size_x = lax.axis_size("gx")
    size_y = lax.axis_size("gy")
    conduct, stored = (conductivity, storage)
    sections = []
    for depth in range(LEVELS_SPLIT):
        if depth > 0:
            conduct = 0.5 * coarsen(conduct)
            stored = coarsen(stored)
        sections.append(face_terms(conduct, stored, 1, 1))
    conduct = 0.5 * coarsen(conduct)
    stored = coarsen(stored)
    whole = gather_whole(jnp.stack([conduct, stored]))
    conduct, stored = (whole[0], whole[1])
    for depth in range(LEVELS_MERGED):
        if depth > 0:
            conduct = 0.5 * coarsen(conduct)
            stored = coarsen(stored)
        sections.append(face_terms(conduct, stored, size_x, size_y))
    return cycle(sections, 0, source, pressure)


def solution(mesh):
    placed = (P("gx", "gy"), P("gx", "gy"), P("gx", "gy"), P("gx", "gy"))
    return jax.shard_map(
        per_device, mesh=mesh, in_specs=placed, out_specs=P("gx", "gy"), check_vma=False
    )
```

profile of v0, /device:TPU:12, one launch (start us, length us, event | category | flops | bytes accessed | tf_op | source)
XLA Modules:
  0.0 519.2 jit_solution(9224058231302290926)
XLA Ops:
  8.2 3.1 collective-permute-start
  12.1 2.4 collective-permute-start.1
  14.5 18.9 %reshape.83 = f32[128,2,128,2]{3,2,1,0:T(8,128)} reshape(f32[256,256]{1,0:T(8,128)} %param.6) | data formatting | bytes 524288 | tf_op jit(solution)/shard_map/reshape | solution.py:29
  33.4 8.0 %reduce_sum.137 = f32[128,128]{1,0:T(8,128)S(1)} reduce(f32[128,2,128,2]{3,2,1,0:T(8,128)} %reshape.83, f32[]{:T(128)} %constant.15.clone.1), dimensions={1,3}, to_apply=%region_2.0 | reduce | flops 49152 | bytes 327684 | tf_op jit(solution)/shard_map/reduce_sum | solution.py:29
  43.7 5.6 %mul.661 = f32[64,2,64,2]{3,2,1,0:T(8,128)} reshape(f32[128,128]{1,0:T(8,128)S(1)} %broadcast_multiply_fusion) | data formatting | bytes 131072 | tf_op jit(solution)/shard_map/mul | solution.py:135
  49.2 18.1 %reshape.82 = f32[128,2,128,2]{3,2,1,0:T(8,128)} reshape(f32[256,256]{1,0:T(8,128)S(1)} %copy-done.25) | data formatting | bytes 524288 | tf_op jit(solution)/shard_map/reshape | solution.py:29
  67.3 8.0 %reduce_sum.136 = f32[128,128]{1,0:T(8,128)S(1)} reduce(f32[128,2,128,2]{3,2,1,0:T(8,128)} %reshape.82, f32[]{:T(128)} %constant.15.clone.1), dimensions={1,3}, to_apply=%region_1.0 | reduce | flops 49152 | bytes 327684 | tf_op jit(solution)/shard_map/reduce_sum | solution.py:29
  75.3 5.6 %reshape.85 = f32[64,2,64,2]{3,2,1,0:T(8,128)} reshape(f32[128,128]{1,0:T(8,128)S(1)} %reduce_sum.136) | data formatting | bytes 131072 | tf_op jit(solution)/shard_map/reshape | solution.py:29
  80.9 2.8 reduce_sum.139
  83.7 2.8 reduce_sum.140
  89.8 14.8 %all_gather.14 = f32[2,128,16]{2,0,1:T(2,128)S(1)} all-gather(f32[2,16,16]{2,0,1:T(2,128)S(1)} %copy.102), channel_id=1, replica_groups=mesh['gx'=8,'gy'=4] {'gx'}, dimensions={1}, use_global_device_ids=true | all-gather | bytes 18432 | tf_op jit(solution)/shard_map/all_gather | solution.py:98
  104.7 8.2 %all_gather.15 = f32[2,128,64]{1,2,0:T(8,128)S(1)} all-gather(f32[2,128,16]{1,2,0:T(8,128)S(1)} %copy.103), channel_id=1, replica_groups=mesh['gx'=8,'gy'=4] {'gy'}, dimensions={2}, use_global_device_ids=true | all-gather | bytes 81920 | tf_op jit(solution)/shard_map/all_gather | solution.py:99
  119.6 3.4 collective-permute-start.7
  122.9 2.5 collective-permute-start.6
  127.5 5.0 collective-permute-start.3
  140.4 3.2 collective-permute-start.9
  146.2 3.7 collective-permute-done.8
  150.0 3.4 collective-permute-start.11
  153.3 2.5 collective-permute-start.10
  162.2 3.6 collective-permute-start.13
  168.4 3.8 collective-permute-done.12
  172.3 2.9 collective-permute-start.15
  175.2 2.9 collective-permute-start.14
  181.6 3.4 collective-permute-start.19
  185.6 18.1 %reshape.81 = f32[128,2,128,2]{3,2,1,0:T(8,128)} reshape(f32[256,256]{1,0:T(8,128)S(1)} %copy.100) | data formatting | bytes 524288 | tf_op jit(solution)/shard_map/reshape | solution.py:29
  203.7 8.0 %reduce_sum.135 = f32[128,128]{1,0:T(8,128)S(1)} reduce(f32[128,2,128,2]{3,2,1,0:T(8,128)} %reshape.81, f32[]{:T(128)} %constant.15.clone.1), dimensions={1,3}, to_apply=%region_0.0 | reduce | flops 49152 | bytes 327684 | tf_op jit(solution)/shard_map/reduce_sum | solution.py:29
  217.6 2.8 reshape_squeeze.6
  221.8 3.0 collective-permute-start.23
  224.8 2.9 collective-permute-start.22
  242.5 3.6 collective-permute-start.26
  248.0 4.8 collective-permute-start.31
  254.1 5.6 %reshape.84 = f32[64,2,64,2]{3,2,1,0:T(8,128)} reshape(f32[128,128]{1,0:T(8,128)S(1)} %fusion.91) | data formatting | bytes 131072 | tf_op jit(solution)/shard_map/reshape | solution.py:29
  259.7 2.9 reduce_sum.138
  272.6 3.6 collective-permute-start.34
  276.9 2.5 collective-permute-done.34
  289.2 3.9 collective-permute-start.38
  295.1 4.8 collective-permute-start.43
  307.3 2.4 collective-permute-done.44
  309.8 4.4 collective-permute-start.47
  316.2 4.6 collective-permute-done.46
  330.3 3.9 collective-permute-start.50
  334.3 2.6 collective-permute-done.50
  337.9 14.2 %all-gather = f32[128,16]{1,0:T(8,128)S(1)} all-gather(f32[16,16]{1,0:T(8,128)S(1)} %reduce_sum.144), channel_id=2, replica_groups=mesh['gx'=8,'gy'=4] {'gx'}, dimensions={0}, use_global_device_ids=true | all-gather | bytes 9216 | tf_op jit(solution)/shard_map/all_gather | solution.py:98
  352.1 7.8 %all-gather.1 = f32[128,64]{0,1:T(8,128)S(1)} all-gather(f32[128,16]{0,1:T(8,128)S(1)} %copy.101), channel_id=3, replica_groups=mesh['gx'=8,'gy'=4] {'gy'}, dimensions={1}, use_global_device_ids=true | all-gather | bytes 40960 | tf_op jit(solution)/shard_map/all_gather | solution.py:99
  361.5 2.8 reshape.90
  389.6 3.4 collective-permute-start.55
  393.0 2.5 collective-permute-start.54
  395.5 4.1 collective-permute-done.54
  409.3 3.9 collective-permute-start.58
  413.2 2.6 collective-permute-done.58
  426.6 3.9 collective-permute-start.62
  430.5 2.8 collective-permute-done.62
  443.1 3.9 collective-permute-start.66
  447.1 2.8 collective-permute-done.66
  459.8 3.9 collective-permute-start.70
  464.0 2.8 collective-permute-done.70
  475.9 3.9 collective-permute-start.74
  480.2 2.8 collective-permute-done.74
  488.1 3.8 collective-permute-done.76
  493.9 3.9 collective-permute-start.78
  497.8 2.4 collective-permute-done.78
  505.3 3.8 collective-permute-done.80
  511.1 3.9 collective-permute-start.82
  515.0 2.4 collective-permute-done.82
  (412 shorter events, 204.9 us)
Async XLA Ops:
  1.5 117.3 %collective-permute-start.5 = (f32[1,256]{0,1:T(8,128)}, f32[1,256]{0,1:T(8,128)}, u32[]{:S(2)}, u32[]{:S(2)}) collective-permute-start(f32[1,256]{0,1:T(8,128)} %copy.93), channel_id=1, source_target_pairs={{4,0},{8,4},{12,8},{16,12},{20,16},{24,20},{28,24},{5,1},{9,5},{13... | collective-permute-start | bytes 3080 | tf_op jit(solution)/shard_map/ppermute | solution.py:22
  4.2 114.6 %collective-permute-start.4 = (f32[1,256]{0,1:T(8,128)}, f32[1,256]{0,1:T(8,128)}, u32[]{:S(2)}, u32[]{:S(2)}) collective-permute-start(f32[1,256]{0,1:T(8,128)} %copy.91), channel_id=1, source_target_pairs={{0,4},{4,8},{8,12},{12,16},{16,20},{20,24},{24,28},{1,5},{5,9},{9,... | collective-permute-start | bytes 3080 | tf_op jit(solution)/shard_map/ppermute | solution.py:21
  8.2 117.3 %collective-permute-start = (f32[1,256]{0,1:T(8,128)}, f32[1,256]{0,1:T(8,128)S(1)}, u32[]{:S(2)}, u32[]{:S(2)}) collective-permute-start(f32[1,256]{0,1:T(8,128)} %copy.80), channel_id=1, source_target_pairs={{0,4},{4,8},{8,12},{12,16},{16,20},{20,24},{24,28},{1,5},{5,9},{9,... | collective-permute-start | bytes 3080 | tf_op jit(solution)/shard_map/ppermute | solution.py:21
  12.1 113.4 %collective-permute-start.1 = (f32[1,256]{0,1:T(8,128)}, f32[1,256]{0,1:T(8,128)S(1)}, u32[]{:S(2)}, u32[]{:S(2)}) collective-permute-start(f32[1,256]{0,1:T(8,128)} %copy.84), channel_id=1, source_target_pairs={{4,0},{8,4},{12,8},{16,12},{20,16},{24,20},{28,24},{5,1},{9,5},{13... | collective-permute-start | bytes 3080 | tf_op jit(solution)/shard_map/ppermute | solution.py:22
  41.4 120.8 %collective-permute-start.16 = (f32[1,128]{1,0:T(1,128)S(1)}, f32[1,128]{1,0:T(1,128)S(1)}, u32[]{:S(2)}, u32[]{:S(2)}) collective-permute-start(f32[1,128]{1,0:T(1,128)S(1)} %get-tuple-element.74), channel_id=1, source_target_pairs={{0,4},{4,8},{8,12},{12,16},{16,20},{20,24},{24,28},{1,5},{5,9},{9,... | collective-permute-start | bytes 1544 | tf_op jit(solution)/shard_map/ppermute | solution.py:21
  119.6 14.7 %collective-permute-start.7 = (f32[258,1]{0,1:T(1,128)S(1)}, f32[258,1]{0,1:T(1,128)S(1)}, u32[]{:S(2)}, u32[]{:S(2)}) collective-permute-start(f32[258,1]{0,1:T(1,128)S(1)} %get-tuple-element.39), channel_id=1, source_target_pairs={{1,0},{2,1},{3,2},{5,4},{6,5},{7,6},{9,8},{10,9},{11,10},{13,12},{... | collective-permute-start | bytes 3104 | tf_op jit(solution)/shard_map/ppermute | solution.py:22
  122.9 13.2 %collective-permute-start.6 = (f32[258,1]{0,1:T(1,128)S(1)}, f32[258,1]{0,1:T(1,128)S(1)}, u32[]{:S(2)}, u32[]{:S(2)}) collective-permute-start(f32[258,1]{0,1:T(1,128)S(1)} %get-tuple-element.38), channel_id=1, source_target_pairs={{0,1},{1,2},{2,3},{4,5},{5,6},{6,7},{8,9},{9,10},{10,11},{12,13},{... | collective-permute-start | bytes 3104 | tf_op jit(solution)/shard_map/ppermute | solution.py:21
  125.5 13.1 %collective-permute-start.2 = (f32[258,1]{0,1:T(1,128)S(1)}, f32[258,1]{0,1:T(1,128)S(1)}, u32[]{:S(2)}, u32[]{:S(2)}) collective-permute-start(f32[258,1]{0,1:T(1,128)S(1)} %get-tuple-element.37), channel_id=1, source_target_pairs={{0,1},{1,2},{2,3},{4,5},{5,6},{6,7},{8,9},{9,10},{10,11},{12,13},{... | collective-permute-start | bytes 3104 | tf_op jit(solution)/shard_map/ppermute | solution.py:21
  127.5 11.2 %collective-permute-start.3 = (f32[258,1]{0,1:T(1,128)S(1)}, f32[258,1]{0,1:T(1,128)S(1)}, u32[]{:S(2)}, u32[]{:S(2)}) collective-permute-start(f32[258,1]{0,1:T(1,128)S(1)} %get-tuple-element.36), channel_id=1, source_target_pairs={{1,0},{2,1},{3,2},{5,4},{6,5},{7,6},{9,8},{10,9},{11,10},{13,12},{... | collective-permute-start | bytes 3104 | tf_op jit(solution)/shard_map/ppermute | solution.py:22
  134.3 31.6 %collective-permute-start.17 = (f32[1,128]{1,0:T(1,128)S(1)}, f32[1,128]{1,0:T(1,128)S(1)}, u32[]{:S(2)}, u32[]{:S(2)}) collective-permute-start(f32[1,128]{1,0:T(1,128)S(1)} %get-tuple-element.73), channel_id=1, source_target_pairs={{4,0},{8,4},{12,8},{16,12},{20,16},{24,20},{28,24},{5,1},{9,5},{13... | collective-permute-start | bytes 1544 | tf_op jit(solution)/shard_map/ppermute | solution.py:22
  136.2 99.0 %collective-permute-start.28 = (f32[1,64]{1,0:T(1,128)}, f32[1,64]{1,0:T(1,128)}, u32[]{:S(2)}, u32[]{:S(2)}) collective-permute-start(f32[1,64]{1,0:T(1,128)} %get-tuple-element.97), channel_id=1, source_target_pairs={{0,4},{4,8},{8,12},{12,16},{16,20},{20,24},{24,28},{1,5},{5,9},{9,... | collective-permute-start | bytes 776 | tf_op jit(solution)/shard_map/ppermute | solution.py:21
  140.4 5.7 %collective-permute-start.9 = (f32[1,256]{0,1:T(8,128)S(1)}, f32[1,256]{0,1:T(8,128)S(1)}, u32[]{:S(2)}, u32[]{:S(2)}) collective-permute-start(f32[1,256]{0,1:T(8,128)S(1)} %get-tuple-element.47), channel_id=1, source_target_pairs={{4,0},{8,4},{12,8},{16,12},{20,16},{24,20},{28,24},{5,1},{9,5},{13... | collective-permute-start | bytes 3080 | tf_op jit(solution)/shard_map/ppermute | solution.py:22
  143.6 6.3 %collective-permute-start.8 = (f32[1,256]{0,1:T(8,128)S(1)}, f32[1,256]{0,1:T(8,128)S(1)}, u32[]{:S(2)}, u32[]{:S(2)}) collective-permute-start(f32[1,256]{0,1:T(8,128)S(1)} %get-tuple-element.46), channel_id=1, source_target_pairs={{0,4},{4,8},{8,12},{12,16},{16,20},{20,24},{24,28},{1,5},{5,9},{9,... | collective-permute-start | bytes 3080 | tf_op jit(solution)/shard_map/ppermute | solution.py:21
  150.0 6.5 %collective-permute-start.11 = (f32[258,1]{0,1:T(1,128)S(1)}, f32[258,1]{0,1:T(1,128)S(1)}, u32[]{:S(2)}, u32[]{:S(2)}) collective-permute-start(f32[258,1]{0,1:T(1,128)S(1)} %get-tuple-element.35), channel_id=1, source_target_pairs={{1,0},{2,1},{3,2},{5,4},{6,5},{7,6},{9,8},{10,9},{11,10},{13,12},{... | collective-permute-start | bytes 3104 | tf_op jit(solution)/shard_map/ppermute | solution.py:22
  153.3 6.4 %collective-permute-start.10 = (f32[258,1]{0,1:T(1,128)S(1)}, f32[258,1]{0,1:T(1,128)S(1)}, u32[]{:S(2)}, u32[]{:S(2)}) collective-permute-start(f32[258,1]{0,1:T(1,128)S(1)} %get-tuple-element.34), channel_id=1, source_target_pairs={{0,1},{1,2},{2,3},{4,5},{5,6},{6,7},{8,9},{9,10},{10,11},{12,13},{... | collective-permute-start | bytes 3104 | tf_op jit(solution)/shard_map/ppermute | solution.py:21
  156.4 81.2 %collective-permute-start.29 = (f32[1,64]{1,0:T(1,128)}, f32[1,64]{1,0:T(1,128)}, u32[]{:S(2)}, u32[]{:S(2)}) collective-permute-start(f32[1,64]{1,0:T(1,128)} %get-tuple-element.96), channel_id=1, source_target_pairs={{4,0},{8,4},{12,8},{16,12},{20,16},{24,20},{28,24},{5,1},{9,5},{13... | collective-permute-start | bytes 776 | tf_op jit(solution)/shard_map/ppermute | solution.py:22
  159.7 116.5 %collective-permute-start.40 = (f32[1,32]{1,0:T(1,128)}, f32[1,32]{1,0:T(1,128)}, u32[]{:S(2)}, u32[]{:S(2)}) collective-permute-start(f32[1,32]{1,0:T(1,128)} %get-tuple-element.117), channel_id=1, source_target_pairs={{0,4},{4,8},{8,12},{12,16},{16,20},{20,24},{24,28},{1,5},{5,9},{9,... | collective-permute-start | bytes 392 | tf_op jit(solution)/shard_map/ppermute | solution.py:21
  162.2 6.1 %collective-permute-start.13 = (f32[1,256]{0,1:T(8,128)S(1)}, f32[1,256]{0,1:T(8,128)S(1)}, u32[]{:S(2)}, u32[]{:S(2)}) collective-permute-start(f32[1,256]{0,1:T(8,128)S(1)} %get-tuple-element.45), channel_id=1, source_target_pairs={{4,0},{8,4},{12,8},{16,12},{20,16},{24,20},{28,24},{5,1},{9,5},{13... | collective-permute-start | bytes 3080 | tf_op jit(solution)/shard_map/ppermute | solution.py:22
  165.9 6.3 %collective-permute-start.12 = (f32[1,256]{0,1:T(8,128)S(1)}, f32[1,256]{0,1:T(8,128)S(1)}, u32[]{:S(2)}, u32[]{:S(2)}) collective-permute-start(f32[1,256]{0,1:T(8,128)S(1)} %get-tuple-element.44), channel_id=1, source_target_pairs={{0,4},{4,8},{8,12},{12,16},{16,20},{20,24},{24,28},{1,5},{5,9},{9,... | collective-permute-start | bytes 3080 | tf_op jit(solution)/shard_map/ppermute | solution.py:21
  172.3 5.9 %collective-permute-start.15 = (f32[258,1]{0,1:T(1,128)S(1)}, f32[258,1]{0,1:T(1,128)S(1)}, u32[]{:S(2)}, u32[]{:S(2)}) collective-permute-start(f32[258,1]{0,1:T(1,128)S(1)} %get-tuple-element.33), channel_id=1, source_target_pairs={{1,0},{2,1},{3,2},{5,4},{6,5},{7,6},{9,8},{10,9},{11,10},{13,12},{... | collective-permute-start | bytes 3104 | tf_op jit(solution)/shard_map/ppermute | solution.py:22
  175.2 6.4 %collective-permute-start.14 = (f32[258,1]{0,1:T(1,128)S(1)}, f32[258,1]{0,1:T(1,128)S(1)}, u32[]{:S(2)}, u32[]{:S(2)}) collective-permute-start(f32[258,1]{0,1:T(1,128)S(1)} %get-tuple-element.32), channel_id=1, source_target_pairs={{0,1},{1,2},{2,3},{4,5},{5,6},{6,7},{8,9},{9,10},{10,11},{12,13},{... | collective-permute-start | bytes 3104 | tf_op jit(solution)/shard_map/ppermute | solution.py:21
  178.2 33.6 %collective-permute-start.18 = (f32[130,1]{1,0:T(8,128)S(1)}, f32[130,1]{1,0:T(8,128)S(1)}, u32[]{:S(2)}, u32[]{:S(2)}) collective-permute-start(f32[130,1]{1,0:T(8,128)S(1)} %get-tuple-element.61), channel_id=1, source_target_pairs={{0,1},{1,2},{2,3},{4,5},{5,6},{6,7},{8,9},{9,10},{10,11},{12,13},{... | collective-permute-start | bytes 1568 | tf_op jit(solution)/shard_map/ppermute | solution.py:21
  181.6 30.2 %collective-permute-start.19 = (f32[130,1]{1,0:T(8,128)S(1)}, f32[130,1]{1,0:T(8,128)S(1)}, u32[]{:S(2)}, u32[]{:S(2)}) collective-permute-start(f32[130,1]{1,0:T(8,128)S(1)} %get-tuple-element.60), channel_id=1, source_target_pairs={{1,0},{2,1},{3,2},{5,4},{6,5},{7,6},{9,8},{10,9},{11,10},{13,12},{... | collective-permute-start | bytes 1568 | tf_op jit(solution)/shard_map/ppermute | solution.py:22
  213.3 7.6 %collective-permute-start.21 = (f32[1,128]{1,0:T(1,128)}, f32[1,128]{1,0:T(1,128)}, u32[]{:S(2)}, u32[]{:S(2)}) collective-permute-start(f32[1,128]{1,0:T(1,128)} %get-tuple-element.72), channel_id=1, source_target_pairs={{4,0},{8,4},{12,8},{16,12},{20,16},{24,20},{28,24},{5,1},{9,5},{13... | collective-permute-start | bytes 1544 | tf_op jit(solution)/shard_map/ppermute | solution.py:22
  215.2 5.7 %collective-permute-start.20 = (f32[1,128]{1,0:T(1,128)}, f32[1,128]{1,0:T(1,128)}, u32[]{:S(2)}, u32[]{:S(2)}) collective-permute-start(f32[1,128]{1,0:T(1,128)} %get-tuple-element.71), channel_id=1, source_target_pairs={{0,4},{4,8},{8,12},{12,16},{16,20},{20,24},{24,28},{1,5},{5,9},{9,... | collective-permute-start | bytes 1544 | tf_op jit(solution)/shard_map/ppermute | solution.py:21
  221.8 6.2 %collective-permute-start.23 = (f32[130,1]{1,0:T(8,128)S(1)}, f32[130,1]{1,0:T(8,128)S(1)}, u32[]{:S(2)}, u32[]{:S(2)}) collective-permute-start(f32[130,1]{1,0:T(8,128)S(1)} %get-tuple-element.59), channel_id=1, source_target_pairs={{1,0},{2,1},{3,2},{5,4},{6,5},{7,6},{9,8},{10,9},{11,10},{13,12},{... | collective-permute-start | bytes 1568 | tf_op jit(solution)/shard_map/ppermute | solution.py:22
  224.8 7.1 %collective-permute-start.22 = (f32[130,1]{1,0:T(8,128)S(1)}, f32[130,1]{1,0:T(8,128)S(1)}, u32[]{:S(2)}, u32[]{:S(2)}) collective-permute-start(f32[130,1]{1,0:T(8,128)S(1)} %get-tuple-element.58), channel_id=1, source_target_pairs={{0,1},{1,2},{2,3},{4,5},{5,6},{6,7},{8,9},{9,10},{10,11},{12,13},{... | collective-permute-start | bytes 1568 | tf_op jit(solution)/shard_map/ppermute | solution.py:21
  228.0 48.3 %collective-permute-start.41 = (f32[1,32]{1,0:T(1,128)}, f32[1,32]{1,0:T(1,128)S(1)}, u32[]{:S(2)}, u32[]{:S(2)}) collective-permute-start(f32[1,32]{1,0:T(1,128)} %get-tuple-element.116), channel_id=1, source_target_pairs={{4,0},{8,4},{12,8},{16,12},{20,16},{24,20},{28,24},{5,1},{9,5},{13... | collective-permute-start | bytes 392 | tf_op jit(solution)/shard_map/ppermute | solution.py:22
  233.3 5.1 collective-permute-start.25
  240.2 7.9 %collective-permute-start.27 = (f32[130,1]{1,0:T(8,128)S(1)}, f32[130,1]{1,0:T(8,128)S(1)}, u32[]{:S(2)}, u32[]{:S(2)}) collective-permute-start(f32[130,1]{1,0:T(8,128)S(1)} %get-tuple-element.57), channel_id=1, source_target_pairs={{1,0},{2,1},{3,2},{5,4},{6,5},{7,6},{9,8},{10,9},{11,10},{13,12},{... | collective-permute-start | bytes 1568 | tf_op jit(solution)/shard_map/ppermute | solution.py:22
  242.5 10.4 %collective-permute-start.26 = (f32[130,1]{1,0:T(8,128)S(1)}, f32[130,1]{1,0:T(8,128)S(1)}, u32[]{:S(2)}, u32[]{:S(2)}) collective-permute-start(f32[130,1]{1,0:T(8,128)S(1)} %get-tuple-element.56), channel_id=1, source_target_pairs={{0,1},{1,2},{2,3},{4,5},{5,6},{6,7},{8,9},{9,10},{10,11},{12,13},{... | collective-permute-start | bytes 1568 | tf_op jit(solution)/shard_map/ppermute | solution.py:21
  246.1 16.4 %collective-permute-start.30 = (f32[66,1]{1,0:T(8,128)S(1)}, f32[66,1]{1,0:T(8,128)S(1)}, u32[]{:S(2)}, u32[]{:S(2)}) collective-permute-start(f32[66,1]{1,0:T(8,128)S(1)} %get-tuple-element.84), channel_id=1, source_target_pairs={{0,1},{1,2},{2,3},{4,5},{5,6},{6,7},{8,9},{9,10},{10,11},{12,13},{... | collective-permute-start | bytes 800 | tf_op jit(solution)/shard_map/ppermute | solution.py:21
  248.0 14.5 %collective-permute-start.31 = (f32[66,1]{1,0:T(8,128)S(1)}, f32[66,1]{1,0:T(8,128)S(1)}, u32[]{:S(2)}, u32[]{:S(2)}) collective-permute-start(f32[66,1]{1,0:T(8,128)S(1)} %get-tuple-element.83), channel_id=1, source_target_pairs={{1,0},{2,1},{3,2},{5,4},{6,5},{7,6},{9,8},{10,9},{11,10},{13,12},{... | collective-permute-start | bytes 800 | tf_op jit(solution)/shard_map/ppermute | solution.py:22
  265.4 4.9 collective-permute-start.32
  270.4 6.5 %collective-permute-start.35 = (f32[66,1]{1,0:T(8,128)S(1)}, f32[66,1]{1,0:T(8,128)S(1)}, u32[]{:S(2)}, u32[]{:S(2)}) collective-permute-start(f32[66,1]{1,0:T(8,128)S(1)} %get-tuple-element.82), channel_id=1, source_target_pairs={{1,0},{2,1},{3,2},{5,4},{6,5},{7,6},{9,8},{10,9},{11,10},{13,12},{... | collective-permute-start | bytes 800 | tf_op jit(solution)/shard_map/ppermute | solution.py:22
  272.6 6.8 %collective-permute-start.34 = (f32[66,1]{1,0:T(8,128)S(1)}, f32[66,1]{1,0:T(8,128)S(1)}, u32[]{:S(2)}, u32[]{:S(2)}) collective-permute-start(f32[66,1]{1,0:T(8,128)S(1)} %get-tuple-element.81), channel_id=1, source_target_pairs={{0,1},{1,2},{2,3},{4,5},{5,6},{6,7},{8,9},{9,10},{10,11},{12,13},{... | collective-permute-start | bytes 800 | tf_op jit(solution)/shard_map/ppermute | solution.py:21
  282.1 4.9 collective-permute-start.36
  287.1 12.9 %collective-permute-start.39 = (f32[66,1]{1,0:T(8,128)S(1)}, f32[66,1]{1,0:T(8,128)S(1)}, u32[]{:S(2)}, u32[]{:S(2)}) collective-permute-start(f32[66,1]{1,0:T(8,128)S(1)} %get-tuple-element.80), channel_id=1, source_target_pairs={{1,0},{2,1},{3,2},{5,4},{6,5},{7,6},{9,8},{10,9},{11,10},{13,12},{... | collective-permute-start | bytes 800 | tf_op jit(solution)/shard_map/ppermute | solution.py:22
  289.2 10.7 %collective-permute-start.38 = (f32[66,1]{1,0:T(8,128)S(1)}, f32[66,1]{1,0:T(8,128)S(1)}, u32[]{:S(2)}, u32[]{:S(2)}) collective-permute-start(f32[66,1]{1,0:T(8,128)S(1)} %get-tuple-element.79), channel_id=1, source_target_pairs={{0,1},{1,2},{2,3},{4,5},{5,6},{6,7},{8,9},{9,10},{10,11},{12,13},{... | collective-permute-start | bytes 800 | tf_op jit(solution)/shard_map/ppermute | solution.py:21
  293.2 8.9 %collective-permute-start.42 = (f32[34,1]{1,0:T(8,128)S(1)}, f32[34,1]{1,0:T(8,128)S(1)}, u32[]{:S(2)}, u32[]{:S(2)}) collective-permute-start(f32[34,1]{1,0:T(8,128)S(1)} %get-tuple-element.107), channel_id=1, source_target_pairs={{0,1},{1,2},{2,3},{4,5},{5,6},{6,7},{8,9},{9,10},{10,11},{12,13},{... | collective-permute-start | bytes 416 | tf_op jit(solution)/shard_map/ppermute | solution.py:21
  295.1 7.0 %collective-permute-start.43 = (f32[34,1]{1,0:T(8,128)S(1)}, f32[34,1]{1,0:T(8,128)S(1)}, u32[]{:S(2)}, u32[]{:S(2)}) collective-permute-start(f32[34,1]{1,0:T(8,128)S(1)} %get-tuple-element.106), channel_id=1, source_target_pairs={{1,0},{2,1},{3,2},{5,4},{6,5},{7,6},{9,8},{10,9},{11,10},{13,12},{... | collective-permute-start | bytes 416 | tf_op jit(solution)/shard_map/ppermute | solution.py:22
  304.9 4.9 collective-permute-start.44
  309.8 6.3 %collective-permute-start.47 = (f32[34,1]{1,0:T(8,128)S(1)}, f32[34,1]{1,0:T(8,128)S(1)}, u32[]{:S(2)}, u32[]{:S(2)}) collective-permute-start(f32[34,1]{1,0:T(8,128)S(1)} %get-tuple-element.105), channel_id=1, source_target_pairs={{1,0},{2,1},{3,2},{5,4},{6,5},{7,6},{9,8},{10,9},{11,10},{13,12},{... | collective-permute-start | bytes 416 | tf_op jit(solution)/shard_map/ppermute | solution.py:22
  314.2 6.6 %collective-permute-start.46 = (f32[34,1]{1,0:T(8,128)S(1)}, f32[34,1]{1,0:T(8,128)S(1)}, u32[]{:S(2)}, u32[]{:S(2)}) collective-permute-start(f32[34,1]{1,0:T(8,128)S(1)} %get-tuple-element.104), channel_id=1, source_target_pairs={{0,1},{1,2},{2,3},{4,5},{5,6},{6,7},{8,9},{9,10},{10,11},{12,13},{... | collective-permute-start | bytes 416 | tf_op jit(solution)/shard_map/ppermute | solution.py:21
  328.4 5.9 %collective-permute-start.51 = (f32[34,1]{1,0:T(8,128)S(1)}, f32[34,1]{1,0:T(8,128)S(1)}, u32[]{:S(2)}, u32[]{:S(2)}) collective-permute-start(f32[34,1]{1,0:T(8,128)S(1)} %get-tuple-element.103), channel_id=1, source_target_pairs={{1,0},{2,1},{3,2},{5,4},{6,5},{7,6},{9,8},{10,9},{11,10},{13,12},{... | collective-permute-start | bytes 416 | tf_op jit(solution)/shard_map/ppermute | solution.py:22
  330.3 6.6 %collective-permute-start.50 = (f32[34,1]{1,0:T(8,128)S(1)}, f32[34,1]{1,0:T(8,128)S(1)}, u32[]{:S(2)}, u32[]{:S(2)}) collective-permute-start(f32[34,1]{1,0:T(8,128)S(1)} %get-tuple-element.102), channel_id=1, source_target_pairs={{0,1},{1,2},{2,3},{4,5},{5,6},{6,7},{8,9},{9,10},{10,11},{12,13},{... | collective-permute-start | bytes 416 | tf_op jit(solution)/shard_map/ppermute | solution.py:21
  389.6 5.8 %collective-permute-start.55 = (f32[34,1]{1,0:T(8,128)S(1)}, f32[34,1]{1,0:T(8,128)S(1)}, u32[]{:S(2)}, u32[]{:S(2)}) collective-permute-start(f32[34,1]{1,0:T(8,128)S(1)} %get-tuple-element.101), channel_id=1, source_target_pairs={{1,0},{2,1},{3,2},{5,4},{6,5},{7,6},{9,8},{10,9},{11,10},{13,12},{... | collective-permute-start | bytes 416 | tf_op jit(solution)/shard_map/ppermute | solution.py:22
  393.0 6.6 %collective-permute-start.54 = (f32[34,1]{1,0:T(8,128)S(1)}, f32[34,1]{1,0:T(8,128)S(1)}, u32[]{:S(2)}, u32[]{:S(2)}) collective-permute-start(f32[34,1]{1,0:T(8,128)S(1)} %get-tuple-element.100), channel_id=1, source_target_pairs={{0,1},{1,2},{2,3},{4,5},{5,6},{6,7},{8,9},{9,10},{10,11},{12,13},{... | collective-permute-start | bytes 416 | tf_op jit(solution)/shard_map/ppermute | solution.py:21
  407.4 5.8 %collective-permute-start.59 = (f32[34,1]{1,0:T(8,128)S(1)}, f32[34,1]{1,0:T(8,128)S(1)}, u32[]{:S(2)}, u32[]{:S(2)}) collective-permute-start(f32[34,1]{1,0:T(8,128)S(1)} %get-tuple-element.99), channel_id=1, source_target_pairs={{1,0},{2,1},{3,2},{5,4},{6,5},{7,6},{9,8},{10,9},{11,10},{13,12},{... | collective-permute-start | bytes 416 | tf_op jit(solution)/shard_map/ppermute | solution.py:22
  409.3 6.6 %collective-permute-start.58 = (f32[34,1]{1,0:T(8,128)S(1)}, f32[34,1]{1,0:T(8,128)S(1)}, u32[]{:S(2)}, u32[]{:S(2)}) collective-permute-start(f32[34,1]{1,0:T(8,128)S(1)} %get-tuple-element.98), channel_id=1, source_target_pairs={{0,1},{1,2},{2,3},{4,5},{5,6},{6,7},{8,9},{9,10},{10,11},{12,13},{... | collective-permute-start | bytes 416 | tf_op jit(solution)/shard_map/ppermute | solution.py:21
  424.7 5.9 %collective-permute-start.63 = (f32[66,1]{1,0:T(8,128)S(1)}, f32[66,1]{1,0:T(8,128)S(1)}, u32[]{:S(2)}, u32[]{:S(2)}) collective-permute-start(f32[66,1]{1,0:T(8,128)S(1)} %get-tuple-element.78), channel_id=1, source_target_pairs={{1,0},{2,1},{3,2},{5,4},{6,5},{7,6},{9,8},{10,9},{11,10},{13,12},{... | collective-permute-start | bytes 800 | tf_op jit(solution)/shard_map/ppermute | solution.py:22
  426.6 6.8 %collective-permute-start.62 = (f32[66,1]{1,0:T(8,128)S(1)}, f32[66,1]{1,0:T(8,128)S(1)}, u32[]{:S(2)}, u32[]{:S(2)}) collective-permute-start(f32[66,1]{1,0:T(8,128)S(1)} %get-tuple-element.77), channel_id=1, source_target_pairs={{0,1},{1,2},{2,3},{4,5},{5,6},{6,7},{8,9},{9,10},{10,11},{12,13},{... | collective-permute-start | bytes 800 | tf_op jit(solution)/shard_map/ppermute | solution.py:21
  441.2 5.9 %collective-permute-start.67 = (f32[66,1]{1,0:T(8,128)S(1)}, f32[66,1]{1,0:T(8,128)S(1)}, u32[]{:S(2)}, u32[]{:S(2)}) collective-permute-start(f32[66,1]{1,0:T(8,128)S(1)} %get-tuple-element.76), channel_id=1, source_target_pairs={{1,0},{2,1},{3,2},{5,4},{6,5},{7,6},{9,8},{10,9},{11,10},{13,12},{... | collective-permute-start | bytes 800 | tf_op jit(solution)/shard_map/ppermute | solution.py:22
  443.1 6.8 %collective-permute-start.66 = (f32[66,1]{1,0:T(8,128)S(1)}, f32[66,1]{1,0:T(8,128)S(1)}, u32[]{:S(2)}, u32[]{:S(2)}) collective-permute-start(f32[66,1]{1,0:T(8,128)S(1)} %get-tuple-element.75), channel_id=1, source_target_pairs={{0,1},{1,2},{2,3},{4,5},{5,6},{6,7},{8,9},{9,10},{10,11},{12,13},{... | collective-permute-start | bytes 800 | tf_op jit(solution)/shard_map/ppermute | solution.py:21
  457.8 6.2 %collective-permute-start.71 = (f32[130,1]{1,0:T(8,128)S(1)}, f32[130,1]{1,0:T(8,128)S(1)}, u32[]{:S(2)}, u32[]{:S(2)}) collective-permute-start(f32[130,1]{1,0:T(8,128)S(1)} %get-tuple-element.55), channel_id=1, source_target_pairs={{1,0},{2,1},{3,2},{5,4},{6,5},{7,6},{9,8},{10,9},{11,10},{13,12},{... | collective-permute-start | bytes 1568 | tf_op jit(solution)/shard_map/ppermute | solution.py:22
  459.8 7.1 %collective-permute-start.70 = (f32[130,1]{1,0:T(8,128)S(1)}, f32[130,1]{1,0:T(8,128)S(1)}, u32[]{:S(2)}, u32[]{:S(2)}) collective-permute-start(f32[130,1]{1,0:T(8,128)S(1)} %get-tuple-element.54), channel_id=1, source_target_pairs={{0,1},{1,2},{2,3},{4,5},{5,6},{6,7},{8,9},{9,10},{10,11},{12,13},{... | collective-permute-start | bytes 1568 | tf_op jit(solution)/shard_map/ppermute | solution.py:21
  474.0 6.2 %collective-permute-start.75 = (f32[130,1]{1,0:T(8,128)S(1)}, f32[130,1]{1,0:T(8,128)S(1)}, u32[]{:S(2)}, u32[]{:S(2)}) collective-permute-start(f32[130,1]{1,0:T(8,128)S(1)} %get-tuple-element.53), channel_id=1, source_target_pairs={{1,0},{2,1},{3,2},{5,4},{6,5},{7,6},{9,8},{10,9},{11,10},{13,12},{... | collective-permute-start | bytes 1568 | tf_op jit(solution)/shard_map/ppermute | solution.py:22
  475.9 7.1 %collective-permute-start.74 = (f32[130,1]{1,0:T(8,128)S(1)}, f32[130,1]{1,0:T(8,128)S(1)}, u32[]{:S(2)}, u32[]{:S(2)}) collective-permute-start(f32[130,1]{1,0:T(8,128)S(1)} %get-tuple-element.52), channel_id=1, source_target_pairs={{0,1},{1,2},{2,3},{4,5},{5,6},{6,7},{8,9},{9,10},{10,11},{12,13},{... | collective-permute-start | bytes 1568 | tf_op jit(solution)/shard_map/ppermute | solution.py:21
  485.6 6.3 %collective-permute-start.76 = (f32[1,256]{0,1:T(8,128)S(1)}, f32[1,256]{0,1:T(8,128)S(1)}, u32[]{:S(2)}, u32[]{:S(2)}) collective-permute-start(f32[1,256]{0,1:T(8,128)S(1)} %get-tuple-element.42), channel_id=1, source_target_pairs={{0,4},{4,8},{8,12},{12,16},{16,20},{20,24},{24,28},{1,5},{5,9},{9,... | collective-permute-start | bytes 3080 | tf_op jit(solution)/shard_map/ppermute | solution.py:21
  492.0 5.8 %collective-permute-start.79 = (f32[258,1]{0,1:T(1,128)S(1)}, f32[258,1]{0,1:T(1,128)S(1)}, u32[]{:S(2)}, u32[]{:S(2)}) collective-permute-start(f32[258,1]{0,1:T(1,128)S(1)} %get-tuple-element.31), channel_id=1, source_target_pairs={{1,0},{2,1},{3,2},{5,4},{6,5},{7,6},{9,8},{10,9},{11,10},{13,12},{... | collective-permute-start | bytes 3104 | tf_op jit(solution)/shard_map/ppermute | solution.py:22
  493.9 6.4 %collective-permute-start.78 = (f32[258,1]{0,1:T(1,128)S(1)}, f32[258,1]{0,1:T(1,128)S(1)}, u32[]{:S(2)}, u32[]{:S(2)}) collective-permute-start(f32[258,1]{0,1:T(1,128)S(1)} %get-tuple-element.30), channel_id=1, source_target_pairs={{0,1},{1,2},{2,3},{4,5},{5,6},{6,7},{8,9},{9,10},{10,11},{12,13},{... | collective-permute-start | bytes 3104 | tf_op jit(solution)/shard_map/ppermute | solution.py:21
  502.8 6.3 %collective-permute-start.80 = (f32[1,256]{0,1:T(8,128)S(1)}, f32[1,256]{0,1:T(8,128)S(1)}, u32[]{:S(2)}, u32[]{:S(2)}) collective-permute-start(f32[1,256]{0,1:T(8,128)S(1)} %get-tuple-element.40), channel_id=1, source_target_pairs={{0,4},{4,8},{8,12},{12,16},{16,20},{20,24},{24,28},{1,5},{5,9},{9,... | collective-permute-start | bytes 3080 | tf_op jit(solution)/shard_map/ppermute | solution.py:21
  509.2 5.8 %collective-permute-start.83 = (f32[258,1]{0,1:T(1,128)S(1)}, f32[258,1]{0,1:T(1,128)S(1)}, u32[]{:S(2)}, u32[]{:S(2)}) collective-permute-start(f32[258,1]{0,1:T(1,128)S(1)} %get-tuple-element.29), channel_id=1, source_target_pairs={{1,0},{2,1},{3,2},{5,4},{6,5},{7,6},{9,8},{10,9},{11,10},{13,12},{... | collective-permute-start | bytes 3104 | tf_op jit(solution)/shard_map/ppermute | solution.py:22
  511.1 6.4 %collective-permute-start.82 = (f32[258,1]{0,1:T(1,128)S(1)}, f32[258,1]{0,1:T(1,128)S(1)}, u32[]{:S(2)}, u32[]{:S(2)}) collective-permute-start(f32[258,1]{0,1:T(1,128)S(1)} %get-tuple-element.28), channel_id=1, source_target_pairs={{0,1},{1,2},{2,3},{4,5},{5,6},{6,7},{8,9},{9,10},{10,11},{12,13},{... | collective-permute-start | bytes 3104 | tf_op jit(solution)/shard_map/ppermute | solution.py:21
  (81 other events, 3185.5 us)
where the time goes:
time: 527 us; the launch traced here: 519 us
  starting transfers between devices  219 us (42%)
  local copies, waits for them, and re-layouts  98.2 us (19%)
  waiting for transfers between devices  79.9 us (15%)
  other arithmetic  73.9 us (14%)
  blocking collectives  45 us (9%)
    ppermute x42, starting transfers between devices, with_halo(): before = lax.ppermute(last, axis, up)  115 us
    ppermute x42, starting transfers between devices, with_halo(): after = lax.ppermute(first, axis, down)  105 us
    ppermute x42, waiting for transfers between devices, with_halo(): before = lax.ppermute(last, axis, up)  78.1 us
    reshape x10, local copies, waits for them, and re-layouts, coarsen(): return grid.reshape(height // 2, 2, breadth // 2, 2).sum(axis=(1, 3))  71.4 us
    reduce_sum x15, other arithmetic, coarsen(): return grid.reshape(height // 2, 2, breadth // 2, 2).sum(axis=(1, 3))  35.1 us
    all_gather x2, blocking collectives, gather_whole(): stacked = lax.all_gather(stacked, 'gx', axis=1, tiled=True)  29 us
    add x23, other arithmetic, jacobi_sweep(): return field + OMEGA * (right_side - operate(field, section)) / section[0]  17.4 us
    all_gather x2, blocking collectives, gather_whole(): return lax.all_gather(stacked, 'gy', axis=2, tiled=True)  16 us
  transfers between devices with their start and end apart: 84, of which 35 were waited for; matrix products, arithmetic and copies ran while one was open for 26% of the time, Pallas kernels for 0%

commit v1 on v0

v1 whole, which is shorter than its diff:
```python
import functools

import jax
import jax.numpy as jnp
from jax import lax
from jax.experimental import pallas as pl
from jax.experimental.pallas import tpu as pltpu
from jax.sharding import PartitionSpec as P

LEVELS_SPLIT = 4
LEVELS_MERGED = 2
COARSE_SWEEPS = 8
OMEGA = 0.8

LOCAL = LEVELS_SPLIT - 1
LEVELS = LEVELS_SPLIT + LEVELS_MERGED
HALO = 32
G = 8
MESH = pl.DeviceIdType.MESH
F32 = jnp.float32


def round_up(n, m):
    return -(-n // m) * m


def iota(shape, dim):
    return lax.broadcasted_iota(jnp.int32, shape, dim)


def ones_where(mask):
    return jnp.where(mask, 1.0, 0.0).astype(jnp.bfloat16)


def parts(x):
    high = x.astype(jnp.bfloat16)
    low = (x - high.astype(F32)).astype(jnp.bfloat16)
    return high, low


def dot(a, b):
    return jnp.dot(a, b, preferred_element_type=F32)


def left(matrix, x):
    high, low = parts(x)
    return dot(matrix, high) + dot(matrix, low)


def right(x, matrix):
    high, low = parts(x)
    return dot(high, matrix) + dot(low, matrix)


class Level:
    def __init__(self, depth, bx, by, nx, ny):
        self.depth = depth
        self.split = depth < LOCAL
        self.nx, self.ny = nx >> depth, ny >> depth
        if self.split:
            self.halo = HALO >> depth
            self.bx, self.by = bx >> depth, by >> depth
            self.rows = self.bx + 2 * self.halo
            self.lanes = round_up(self.by + 2 * self.halo, 128)
        else:
            self.halo = 0
            self.bx, self.by = self.nx, self.ny
            self.rows = self.nx
            self.lanes = round_up(self.ny, 128)
        for step in (32, 16, 8):
            if self.rows % step == 0:
                self.step = step
                break
        if self.lanes == 128:
            for step in (128, 80, 64):
                if self.rows % step == 0:
                    self.step = step
                    break

    def scratch(self):
        tall = pltpu.VMEM((self.rows + 2 * G, self.lanes), F32)
        flat = pltpu.VMEM((self.rows, self.lanes), F32)
        return [pltpu.VMEM((7, self.rows, self.lanes), F32), tall, tall, tall, flat, flat]

    def inside(self, start, count, mx, my):
        shape = (count, self.lanes)
        row = iota(shape, 0) + start - self.halo
        lane = iota(shape, 1)
        if not self.split:
            return lane < self.ny
        col = jnp.where(lane >= self.lanes - self.halo, lane - self.lanes, lane)
        row = row + mx * self.bx
        gap = (lane >= self.by + self.halo) & (lane < self.lanes - self.halo)
        col = col + my * self.by
        return (row >= 0) & (row < self.nx) & (col >= 0) & (col < self.ny) & ~gap


def neighbours(win, count, lanes):
    mid = win[G : G + count]
    size = count + 2 * G
    up = pltpu.roll(win, 1, 0)[G : G + count]
    down = pltpu.roll(win, size - 1, 0)[G : G + count]
    before = pltpu.roll(mid, 1, 1)
    after = pltpu.roll(mid, lanes - 1, 1)
    return mid, up, down, before, after


def loop(start, count, step, body):
    total = count // step
    if total == 1:
        body(start)
    else:
        pl.loop(0, total)(lambda i: body(pl.multiple_of(start + i * step, 8)))


def setup(level, mx, my, k_ref, s_ref, a_ref, source=None):
    count = level.step

    def body(r):
        mid, up, down, before, after = neighbours(
            k_ref[pl.ds(r, count + 2 * G), :], count, level.lanes
        )
        inside = level.inside(r, count, mx, my)
        if not level.split:
            lane = iota(mid.shape, 1)
            before = jnp.where(lane == 0, 0.0, before)
            after = jnp.where(lane == level.lanes - 1, 0.0, after)
        west, east = 0.5 * (mid + up), 0.5 * (mid + down)
        south, north = 0.5 * (mid + before), 0.5 * (mid + after)
        rows = pl.ds(r, count)
        diag = s_ref[rows, :] + west + east + south + north
        c = jnp.where(inside, OMEGA / diag, 0.0)
        a_ref[0, rows, :] = c * west
        a_ref[1, rows, :] = c * east
        if level.split:
            a_ref[2, rows, :] = c * south
            a_ref[3, rows, :] = c * north
        else:
            a_ref[2, rows, :] = jnp.where(lane == 0, 0.0, c * south)
            a_ref[3, rows, :] = jnp.where(lane == level.ny - 1, 0.0, c * north)
        a_ref[5, rows, :] = c
        a_ref[6, rows, :] = diag * (1.0 / OMEGA)
        if source is not None:
            a_ref[4, rows, :] = c * source[rows_of(r, count), :]

    loop(0, level.rows, count, body)


def rows_of(r, count):
    return pl.ds(r + G, count)


def smooth(level, src, a_ref, put, start=0, total=None):
    count = level.step

    def body(r):
        mid, up, down, before, after = neighbours(
            src[pl.ds(r, count + 2 * G), :], count, level.lanes
        )
        rows = pl.ds(r, count)
        new = (1.0 - OMEGA) * mid + a_ref[4, rows, :]
        new = new + (a_ref[0, rows, :] * up + a_ref[1, rows, :] * down)
        new = new + (a_ref[2, rows, :] * before + a_ref[3, rows, :] * after)
        put(r, rows, mid, new)

    loop(start, level.rows if total is None else total, count, body)


def sweep(level, src, dst, a_ref, start=0, total=None):
    def put(r, rows, mid, new):
        dst[rows_of(r, level.step), :] = new

    smooth(level, src, a_ref, put, start, total)


def residual(level, src, dst, a_ref):
    def put(r, rows, mid, new):
        dst[rows, :] = (new - mid) * a_ref[6, rows, :]

    smooth(level, src, a_ref, put)


def lane_map(fine, coarse, lane):
    half = lane // 2
    if fine.split:
        shift = coarse.lanes - fine.lanes // 2
        half = jnp.where(lane >= fine.lanes - fine.halo, half + shift, half)
    return half


def coarsen(fine, coarse, x):
    shape = (fine.lanes, coarse.lanes)
    cols = ones_where(lane_map(fine, coarse, iota(shape, 0)) == iota(shape, 1))
    shape = (coarse.rows, fine.rows)
    rows = ones_where(iota(shape, 0) == iota(shape, 1) // 2)
    return left(rows, right(x, cols))


def prolong(fine, coarse, mx, my, x):
    shape = (coarse.lanes, fine.lanes)
    lane = iota(shape, 1)
    if fine.split and not coarse.split:
        col = jnp.where(lane >= fine.lanes - fine.halo, lane - fine.lanes, lane)
        gap = (lane >= fine.by + fine.halo) & (lane < fine.lanes - fine.halo)
        target = jnp.where(gap, -2, col + my * fine.by + 2 * coarse.lanes) // 2 - coarse.lanes
        target = jnp.where(gap, -1, target)
    else:
        target = lane_map(fine, coarse, lane)
    cols = ones_where(iota(shape, 0) == target)
    shape = (fine.rows, coarse.rows)
    row = iota(shape, 0)
    if fine.split and not coarse.split:
        row = row - fine.halo + mx * fine.bx
        row = (row + 2 * fine.rows) // 2 - fine.rows
    else:
        row = row // 2
    rows = ones_where(row == iota(shape, 1))
    return left(rows, right(x, cols))


def block_sum(x, first, count, factor, columns, place, lanes):
    shape = (count, x.shape[0])
    row = iota(shape, 1) - first
    rows = ones_where((row >= 0) & (row < count * factor) & ((row + factor) // factor - 1 == iota(shape, 0)))
    shape = (x.shape[1], lanes)
    lane = iota(shape, 0)
    cols = ones_where((lane < columns) & (lane // factor + place == iota(shape, 1)))
    return left(rows, right(x, cols))


def kernel(levels, dx, dy, *refs):
    p_hbm, s_hbm, k_hbm, st_hbm, out_ref = refs[:5]
    ext, strip_l, strip_r, halo_l, halo_r, ga, gb, gca, gcb = refs[5:14]
    held = []
    refs = refs[14:]
    for _ in levels:
        held.append(refs[:6])
        refs = refs[6:]
    load_sem, halo_send, halo_recv, y_send, y_recv, x_send, x_recv = refs

    mx, my = lax.axis_index("gx"), lax.axis_index("gy")
    top = levels[0]
    bx, by = top.bx, top.by
    own = pl.ds(G + HALO, bx)

    loads = []
    for i, ref in enumerate((p_hbm, s_hbm, k_hbm, st_hbm)):
        loads.append(pltpu.make_async_copy(ref, ext.at[i, own, pl.ds(0, by)], load_sem.at[i]))
        loads[-1].start()

    barrier = pltpu.get_barrier_semaphore()
    corners = []
    for sx in (-1, 1):
        for sy in (-1, 1):
            ok = (mx + sx >= 0) & (mx + sx < dx) & (my + sy >= 0) & (my + sy < dy)
            corners.append((sx, sy, ok))
    for d in range(1, dx):
        pl.semaphore_signal(barrier, inc=1, device_id=(lax.rem(mx + d, dx), my), device_id_type=MESH)
    for d in range(1, dy):
        pl.semaphore_signal(barrier, inc=1, device_id=(mx, lax.rem(my + d, dy)), device_id_type=MESH)
    for sx, sy, ok in corners:
        @pl.when(ok)
        def _():
            pl.semaphore_signal(barrier, inc=1, device_id=(mx + sx, my + sy), device_id_type=MESH)

    zero = jnp.zeros((G, top.lanes), F32)
    for i in (0, 2):
        ext[i, 0:G, :] = zero
        ext[i, G + top.rows :, :] = zero
    for level, (a, v, u, k, s, r) in zip(levels, held):
        for ref in (v, u, k):
            ref[0:G, :] = jnp.zeros((G, level.lanes), F32)
            ref[G + level.rows :, :] = jnp.zeros((G, level.lanes), F32)

    for copy in loads:
        copy.wait()

    lane = iota((bx, 128), 1)
    slot = lane // HALO
    for dst, first, at in ((strip_l, 0, 0), (strip_r, by - 128, 128 - HALO)):
        packed = None
        for i in range(4):
            x = ext[i, own, pl.ds(first, 128)]
            turn = (HALO * i - at) % 128
            if turn:
                x = pltpu.roll(x, turn, 1)
            packed = x if packed is None else jnp.where(slot == i, x, packed)
        dst[...] = packed

    corner_count = sum(jnp.where(ok, 1, 0) for _, _, ok in corners)
    pl.semaphore_wait(barrier, dx - 1 + dy - 1 + corner_count)

    halos = []
    n = 0
    for sx in (-1, 0, 1):
        for sy in (-1, 0, 1):
            if sx == 0 and sy == 0:
                continue
            ok = (mx + sx >= 0) & (mx + sx < dx) & (my + sy >= 0) & (my + sy < dy)
            back = (mx - sx >= 0) & (mx - sx < dx) & (my - sy >= 0) & (my - sy < dy)
            if sy == 0:
                first = G + HALO if sx < 0 else G + bx
                there = G + HALO + bx if sx < 0 else G
                src = ext.at[:, pl.ds(first, HALO), pl.ds(0, by)]
                dst = ext.at[:, pl.ds(there, HALO), pl.ds(0, by)]
            else:
                mine, theirs = (strip_l, halo_r) if sy < 0 else (strip_r, halo_l)
                if sx == 0:
                    src, dst = mine, theirs.at[pl.ds(HALO, bx)]
                elif sx < 0:
                    src, dst = mine.at[pl.ds(0, HALO)], theirs.at[pl.ds(HALO + bx, HALO)]
                else:
                    src, dst = mine.at[pl.ds(bx - HALO, HALO)], theirs.at[pl.ds(0, HALO)]
            copy = pltpu.make_async_remote_copy(
                src_ref=src, dst_ref=dst, send_sem=halo_send.at[n], recv_sem=halo_recv.at[n],
                device_id=(mx + sx, my + sy), device_id_type=MESH,
            )
            halos.append((copy, ok, back))
            n += 1
    for copy, ok, _ in halos:
        pl.when(ok)(copy.start)

    whole = levels[LOCAL]
    factor = 1 << LOCAL
    gx_rows, gy_cols = bx // factor, by // factor
    place = my * gy_cols
    sends = []

    def over_gy(buffer, base):
        copies = []
        for d in range(1, dy):
            copies.append(pltpu.make_async_remote_copy(
                src_ref=buffer.at[my], dst_ref=buffer.at[my],
                send_sem=y_send.at[base + d], recv_sem=y_recv.at[base + d],
                device_id=(mx, lax.rem(my + d, dy)), device_id_type=MESH,
            ))
            copies[-1].start()
        sends.extend(copies)
        return copies

    def over_gx(part, base):
        copies = []
        for d in range(1, dx):
            copies.append(pltpu.make_async_remote_copy(
                src_ref=part, dst_ref=part,
                send_sem=x_send.at[base + d], recv_sem=x_recv.at[base + d],
                device_id=(lax.rem(mx + d, dx), my), device_id_type=MESH,
            ))
            copies[-1].start()
        sends.extend(copies)
        return copies

    for i, scale in ((0, 0.5 ** LOCAL), (1, 1.0)):
        x = ext[2 + i, own, pl.ds(0, by)]
        gca[my, i] = scale * block_sum(x, 0, gx_rows, factor, by, place, whole.lanes)
    coef_y = over_gy(gca, 0)

    for copy, _, back in halos:
        pl.when(back)(copy.wait_recv)

    tile = pl.ds(top.lanes - 128, 128)
    lane = iota((HALO, 128), 1)

    @pl.loop(0, top.rows // HALO)
    def _(i):
        r = pl.multiple_of(i * HALO, 8)
        inside = top.inside(r, HALO, mx, my)[:, top.lanes - 128 :]
        lower, upper = halo_l[pl.ds(r, HALO), :], halo_r[pl.ds(r, HALO), :]
        for j in range(4):
            turn_l, turn_r = (128 - HALO - HALO * j) % 128, (-HALO * j) % 128
            x = pltpu.roll(lower, turn_l, 1) if turn_l else lower
            y = pltpu.roll(upper, turn_r, 1) if turn_r else upper
            x = jnp.where(lane < HALO, y, x)
            ext[j, pl.ds(r + G, HALO), tile] = jnp.where(inside, x, 0.0)

    for edge, first in ((mx == 0, G), (mx == dx - 1, G + HALO + bx)):
        @pl.when(edge)
        def _():
            for j in range(4):
                ext[j, pl.ds(first, HALO), pl.ds(0, by)] = jnp.zeros((HALO, by), F32)

    setup(top, mx, my, ext.at[2], ext.at[3, pl.ds(G, top.rows)], held[0][0], ext.at[1])

    for copy in coef_y:
        copy.wait_recv()
    gcb[:, pl.ds(pl.multiple_of(mx * gx_rows, 8), gx_rows), :] = functools.reduce(
        lambda x, y: x + y, [gca[j] for j in range(dy)]
    )
    coef_x = over_gx(gcb.at[:, pl.ds(pl.multiple_of(mx * gx_rows, 8), gx_rows)], 0)

    def inner(level, ref):
        return ref[pl.ds(G, level.rows), :]

    for depth in range(LOCAL):
        level = levels[depth]
        a, v, u, k, s, res = held[depth]
        if depth == 0:
            sweep(level, ext.at[0], v, a)
        else:
            fine = levels[depth - 1]
            fk, fs = (ext.at[2], ext.at[3, pl.ds(G, top.rows)]) if depth == 1 else held[depth - 1][3:5]
            k[pl.ds(G, level.rows), :] = 0.5 * coarsen(fine, level, inner(fine, fk))
            s[...] = coarsen(fine, level, fs[...])
            setup(level, mx, my, k, s, a)
            first = a[5] * coarsen(fine, level, held[depth - 1][5][...])
            a[4] = first
            v[pl.ds(G, level.rows), :] = first
        sweep(level, v, u, a)
        residual(level, u, res, a)

    last = levels[LOCAL - 1]
    ga[my] = block_sum(held[LOCAL - 1][5][...], last.halo, gx_rows, 2, last.by, place, whole.lanes)
    side_y = over_gy(ga, dy)

    for copy in coef_x:
        copy.wait_recv()
    for depth in range(LOCAL, LEVELS):
        level = levels[depth]
        a, v, u, k, s, res = held[depth]
        if depth == LOCAL:
            k[pl.ds(G, level.rows), :] = gcb[0]
            s[...] = gcb[1]
        else:
            fine = levels[depth - 1]
            k[pl.ds(G, level.rows), :] = 0.5 * coarsen(fine, level, inner(fine, held[depth - 1][3]))
            s[...] = coarsen(fine, level, held[depth - 1][4][...])
        setup(level, mx, my, k, s, a)

    for copy in side_y:
        copy.wait_recv()
    part = pl.ds(pl.multiple_of(mx * gx_rows, 8), gx_rows)
    gb[part, :] = functools.reduce(lambda x, y: x + y, [ga[j] for j in range(dy)])
    side_x = over_gx(gb.at[part], dx)
    for copy in side_x:
        copy.wait_recv()

    for depth in range(LOCAL, LEVELS):
        level = levels[depth]
        a, v, u, k, s, res = held[depth]
        side = gb[...] if depth == LOCAL else coarsen(levels[depth - 1], level, held[depth - 1][5][...])
        first = a[5] * side
        a[4] = first
        v[pl.ds(G, level.rows), :] = first
        if depth < LEVELS - 1:
            sweep(level, v, u, a)
            residual(level, u, res, a)
        else:
            for i in range(COARSE_SWEEPS - 1):
                sweep(level, *((v, u) if i % 2 == 0 else (u, v)), a)
            if COARSE_SWEEPS % 2:
                u[...] = v[...]

    for depth in reversed(range(LEVELS - 1)):
        level, below = levels[depth], levels[depth + 1]
        a, v, u, k, s, res = held[depth]
        u[pl.ds(G, level.rows), :] += prolong(level, below, mx, my, inner(below, held[depth + 1][2]))
        if depth:
            sweep(level, u, v, a)
            sweep(level, v, u, a)
        else:
            step = level.step
            sweep(level, u, v, a, HALO - step, bx + 2 * step)

            def put(r, rows, mid, new):
                out_ref[pl.ds(pl.multiple_of(r - HALO, 8), step), :] = new[:, :by]

            smooth(level, v, a, put, HALO, bx)

    for copy, ok, _ in halos:
        pl.when(ok)(copy.wait_send)
    for copy in sends:
        copy.wait_send()


def per_device(nx, ny, pressure, source, conductivity, storage):
    dx, dy = lax.axis_size("gx"), lax.axis_size("gy")
    bx, by = pressure.shape
    levels = [Level(depth, bx, by, nx, ny) for depth in range(LEVELS)]
    top, whole = levels[0], levels[LOCAL]
    rows = bx >> LOCAL
    scratch = [
        pltpu.VMEM((4, top.rows + 2 * G, top.lanes), F32),
        pltpu.VMEM((bx, 128), F32),
        pltpu.VMEM((bx, 128), F32),
        pltpu.VMEM((top.rows, 128), F32),
        pltpu.VMEM((top.rows, 128), F32),
        pltpu.VMEM((dy, rows, whole.lanes), F32),
        pltpu.VMEM((whole.rows, whole.lanes), F32),
        pltpu.VMEM((dy, 2, rows, whole.lanes), F32),
        pltpu.VMEM((2, whole.rows, whole.lanes), F32),
    ]
    for level in levels:
        scratch += level.scratch()
    scratch += [
        pltpu.SemaphoreType.DMA((4,)),
        pltpu.SemaphoreType.DMA((8,)),
        pltpu.SemaphoreType.DMA((8,)),
        pltpu.SemaphoreType.DMA((2 * dy,)),
        pltpu.SemaphoreType.DMA((2 * dy,)),
        pltpu.SemaphoreType.DMA((2 * dx,)),
        pltpu.SemaphoreType.DMA((2 * dx,)),
    ]
    return pl.pallas_call(
        functools.partial(kernel, levels, dx, dy),
        out_shape=jax.ShapeDtypeStruct((bx, by), F32),
        in_specs=[pl.BlockSpec(memory_space=pl.ANY)] * 4,
        out_specs=pl.BlockSpec(memory_space=pltpu.VMEM),
        scratch_shapes=scratch,
        compiler_params=pltpu.CompilerParams(
            collective_id=0, has_side_effects=True, vmem_limit_bytes=48 * 2**20
        ),
    )(pressure, source, conductivity, storage)


def solution(mesh):
    placed = (P("gx", "gy"), P("gx", "gy"), P("gx", "gy"), P("gx", "gy"))

    def run(pressure, source, conductivity, storage):
        nx, ny = pressure.shape
        return jax.shard_map(
            functools.partial(per_device, nx, ny),
            mesh=mesh, in_specs=placed, out_specs=P("gx", "gy"), check_vma=False,
        )(pressure, source, conductivity, storage)

    return run
```

time: 527 us -> 43.7 us (0.08)
  the two profiles are of different devices: /device:TPU:12 before, /device:TPU:1 now
where the time goes in v1:
time: 43.7 us; the launch traced here: 43.3 us
  Pallas kernels  38.8 us (89%)
  local copies, waits for them, and re-layouts  4.5 us (10%)
    pallas_call x1, Pallas kernels, per_device(): pl.pallas_call(functools.partial(kernel, levels, dx, dy), out_shape=jax.S...  38.8 us
    unnamed x9, local copies, waits for them, and re-layouts  4.5 us

profile of v1, /device:TPU:1, one launch (start us, length us, event | category | flops | bytes accessed | tf_op | source)
XLA Modules:
  0.0 43.3 jit_solution(15749607549690291491)
XLA Ops:
  0.0 0.0 copy-start
  0.0 0.9 %copy-done = f32[256,256]{1,0:T(8,128)S(1)} copy-done((f32[256,256]{1,0:T(8,128)S(1)}, f32[256,256]{1,0:T(8,128)}, u32[]{:S(2)}) %copy-start) | copy-done | bytes 262168
  1.0 0.0 copy-start.1
  1.0 0.9 %copy-done.1 = f32[256,256]{1,0:T(8,128)S(1)} copy-done((f32[256,256]{1,0:T(8,128)S(1)}, f32[256,256]{1,0:T(8,128)}, u32[]{:S(2)}) %copy-start.1) | copy-done | bytes 262168
  1.9 0.0 copy-start.2
  1.9 0.9 %copy-done.2 = f32[256,256]{1,0:T(8,128)S(1)} copy-done((f32[256,256]{1,0:T(8,128)S(1)}, f32[256,256]{1,0:T(8,128)}, u32[]{:S(2)}) %copy-start.2) | copy-done | bytes 262168
  2.9 0.0 copy-start.3
  2.9 0.9 %copy-done.3 = f32[256,256]{1,0:T(8,128)S(1)} copy-done((f32[256,256]{1,0:T(8,128)S(1)}, f32[256,256]{1,0:T(8,128)}, u32[]{:S(2)}) %copy-start.3) | copy-done | bytes 262168
  3.8 38.8 %shard_map.46 = f32[256,256]{1,0:T(8,128)S(1)} custom-call(f32[256,256]{1,0:T(8,128)S(1)} %copy-done, f32[256,256]{1,0:T(8,128)S(1)} %copy-done.1, f32[256,256]{1,0:T(8,128)S(1)} %copy-done.2, f32[256,256]{1,0:T(8,128)S(1)} %copy-done.3), custom_call_target="tpu_custom_call" | custom-call | tf_op jit(solution)/shard_map/pallas_call | solution.py:503
  42.6 0.7 %copy.6 = f32[256,256]{1,0:T(8,128)} copy(f32[256,256]{1,0:T(8,128)S(1)} %shard_map.46) | data formatting | bytes 524288
Async XLA Ops:
  0.0 0.9 %copy-start = (f32[256,256]{1,0:T(8,128)S(1)}, f32[256,256]{1,0:T(8,128)}, u32[]{:S(2)}) copy-start(f32[256,256]{1,0:T(8,128)} %refs_0_.1) | copy-start | bytes 786436
  1.0 0.9 %copy-start.1 = (f32[256,256]{1,0:T(8,128)S(1)}, f32[256,256]{1,0:T(8,128)}, u32[]{:S(2)}) copy-start(f32[256,256]{1,0:T(8,128)} %refs_1_.1) | copy-start | bytes 786436
  1.9 0.9 %copy-start.2 = (f32[256,256]{1,0:T(8,128)S(1)}, f32[256,256]{1,0:T(8,128)}, u32[]{:S(2)}) copy-start(f32[256,256]{1,0:T(8,128)} %refs_2_.1) | copy-start | bytes 786436
  2.9 0.9 %copy-start.3 = (f32[256,256]{1,0:T(8,128)S(1)}, f32[256,256]{1,0:T(8,128)}, u32[]{:S(2)}) copy-start(f32[256,256]{1,0:T(8,128)} %refs_3_.1) | copy-start | bytes 786436

commit v2 on v1

--- a/solution.py
+++ b/solution.py
@@ -106,11 +106,8 @@
 
 
 def loop(start, count, step, body):
-    total = count // step
-    if total == 1:
-        body(start)
-    else:
-        pl.loop(0, total)(lambda i: body(pl.multiple_of(start + i * step, 8)))
+    for i in range(count // step):
+        body(start + i * step)
 
 
 def setup(level, mx, my, k_ref, s_ref, a_ref, source=None):
@@ -462,7 +459,7 @@
             sweep(level, u, v, a, HALO - step, bx + 2 * step)
 
             def put(r, rows, mid, new):
-                out_ref[pl.ds(pl.multiple_of(r - HALO, 8), step), :] = new[:, :by]
+                out_ref[pl.ds(r - HALO, step), :] = new[:, :by]
 
             smooth(level, v, a, put, HALO, bx)
 
@@ -503,11 +500,11 @@
     return pl.pallas_call(
         functools.partial(kernel, levels, dx, dy),
         out_shape=jax.ShapeDtypeStruct((bx, by), F32),
-        in_specs=[pl.BlockSpec(memory_space=pl.ANY)] * 4,
+        in_specs=[pl.BlockSpec(memory_space=pltpu.HBM)] * 4,
         out_specs=pl.BlockSpec(memory_space=pltpu.VMEM),
         scratch_shapes=scratch,
         compiler_params=pltpu.CompilerParams(
-            collective_id=0, has_side_effects=True, vmem_limit_bytes=48 * 2**20
+            collective_id=0, has_side_effects=True, vmem_limit_bytes=62 * 2**20
         ),
     )(pressure, source, conductivity, storage)
 

time: 43.7 us -> 35.5 us (0.81)
  Pallas kernels: 38.8 us -> 33.4 us
  local copies, waits for them, and re-layouts: 4.5 us -> 1.67 us
    pallas_call x1, Pallas kernels: 38.8 us -> 33.4 us  [per_device(): pl.pallas_call(functools.partial(kernel, levels, dx, dy), out_shape=jax.S...]
    unnamed x9 -> x1, local copies, waits for them, and re-layouts: 4.5 us -> 1.67 us
where the time goes in v2:
time: 35.5 us; the launch traced here: 35.1 us
  Pallas kernels  33.4 us (94%)
  local copies, waits for them, and re-layouts  1.67 us (5%)
    pallas_call x1, Pallas kernels, per_device(): pl.pallas_call(functools.partial(kernel, levels, dx, dy), out_shape=jax.S...  33.4 us
    unnamed x1, local copies, waits for them, and re-layouts  1.67 us

profile of v2, /device:TPU:1, one launch (start us, length us, event | category | flops | bytes accessed | tf_op | source)
XLA Modules:
  0.0 35.1 jit_solution(9937134563711910196)
XLA Ops:
  0.0 33.4 %shard_map.46 = f32[256,256]{1,0:T(8,128)} custom-call(f32[256,256]{1,0:T(8,128)} %refs_0_.1, f32[256,256]{1,0:T(8,128)} %refs_1_.1, f32[256,256]{1,0:T(8,128)} %refs_2_.1, f32[256,256]{1,0:T(8,128)} %refs_3_.1), custom_call_target="tpu_custom_call" | custom-call | tf_op jit(solution)/shard_map/pallas_call | solution.py:500
  33.4 1.7 %copy.6 = f32[256,256]{1,0:T(8,128)} copy(f32[256,256]{1,0:T(8,128)} %shard_map.46) | data formatting | bytes 524288

commit v3 on v2

--- a/solution.py
+++ b/solution.py
@@ -50,6 +50,25 @@
 def right(x, matrix):
     high, low = parts(x)
     return dot(high, matrix) + dot(low, matrix)
+
+
+def put_tiles(ref, rows, x):
+    for t in range(x.shape[1] // 128):
+        ref[t, rows, :] = x[:, 128 * t : 128 * t + 128]
+
+
+def pair_rows(ref):
+    tiles, rows, _ = ref.shape
+    first, second = pl.ds(0, rows // 2, stride=2), pl.ds(1, rows // 2, stride=2)
+    return jnp.concatenate([ref[t, first, :] + ref[t, second, :] for t in range(tiles)], axis=1)
+
+
+def repeat_rows(ref, x):
+    tiles, rows, _ = ref.shape
+    for t in range(tiles):
+        part = x[:, 128 * t : 128 * t + 128]
+        ref[t, pl.ds(0, rows // 2, stride=2), :] = part
+        ref[t, pl.ds(1, rows // 2, stride=2), :] = part
 
 
 class Level:
@@ -80,7 +99,11 @@
     def scratch(self):
         tall = pltpu.VMEM((self.rows + 2 * G, self.lanes), F32)
         flat = pltpu.VMEM((self.rows, self.lanes), F32)
-        return [pltpu.VMEM((7, self.rows, self.lanes), F32), tall, tall, tall, flat, flat]
+        tiled = (self.lanes // 128, self.rows, 128)
+        return [
+            pltpu.VMEM((7, self.rows, self.lanes), F32), tall, tall, tall, flat,
+            pltpu.VMEM(tiled, F32), pltpu.VMEM((2, *tiled), F32),
+        ]
 
     def inside(self, start, count, mx, my):
         shape = (count, self.lanes)
@@ -110,14 +133,14 @@
         body(start + i * step)
 
 
-def setup(level, mx, my, k_ref, s_ref, a_ref, source=None):
+def setup(level, k_ref, s_ref, a_ref, pairs=None, source=None):
     count = level.step
 
     def body(r):
         mid, up, down, before, after = neighbours(
             k_ref[pl.ds(r, count + 2 * G), :], count, level.lanes
         )
-        inside = level.inside(r, count, mx, my)
+        inside = mid > 0.0
         if not level.split:
             lane = iota(mid.shape, 1)
             before = jnp.where(lane == 0, 0.0, before)
@@ -125,7 +148,8 @@
         west, east = 0.5 * (mid + up), 0.5 * (mid + down)
         south, north = 0.5 * (mid + before), 0.5 * (mid + after)
         rows = pl.ds(r, count)
-        diag = s_ref[rows, :] + west + east + south + north
+        stored = s_ref[rows, :]
+        diag = stored + west + east + south + north
         c = jnp.where(inside, OMEGA / diag, 0.0)
         a_ref[0, rows, :] = c * west
         a_ref[1, rows, :] = c * east
@@ -137,6 +161,9 @@
             a_ref[3, rows, :] = jnp.where(lane == level.ny - 1, 0.0, c * north)
         a_ref[5, rows, :] = c
         a_ref[6, rows, :] = diag * (1.0 / OMEGA)
+        if pairs is not None:
+            put_tiles(pairs.at[0], rows, mid)
+            put_tiles(pairs.at[1], rows, stored)
         if source is not None:
             a_ref[4, rows, :] = c * source[rows_of(r, count), :]
 
@@ -172,7 +199,7 @@
 
 def residual(level, src, dst, a_ref):
     def put(r, rows, mid, new):
-        dst[rows, :] = (new - mid) * a_ref[6, rows, :]
+        put_tiles(dst, rows, (new - mid) * a_ref[6, rows, :])
 
     smooth(level, src, a_ref, put)
 
@@ -185,34 +212,23 @@
     return half
 
 
-def coarsen(fine, coarse, x):
+def matrices(fine, coarse, my):
     shape = (fine.lanes, coarse.lanes)
-    cols = ones_where(lane_map(fine, coarse, iota(shape, 0)) == iota(shape, 1))
-    shape = (coarse.rows, fine.rows)
-    rows = ones_where(iota(shape, 0) == iota(shape, 1) // 2)
-    return left(rows, right(x, cols))
-
-
-def prolong(fine, coarse, mx, my, x):
+    lane, there = iota(shape, 0), iota(shape, 1)
+    if fine.split and not coarse.split:
+        down = (lane < fine.by) & (lane // 2 + my * (fine.by // 2) == there)
+    else:
+        down = lane_map(fine, coarse, lane) == there
     shape = (coarse.lanes, fine.lanes)
-    lane = iota(shape, 1)
+    there, lane = iota(shape, 0), iota(shape, 1)
     if fine.split and not coarse.split:
         col = jnp.where(lane >= fine.lanes - fine.halo, lane - fine.lanes, lane)
         gap = (lane >= fine.by + fine.halo) & (lane < fine.lanes - fine.halo)
-        target = jnp.where(gap, -2, col + my * fine.by + 2 * coarse.lanes) // 2 - coarse.lanes
-        target = jnp.where(gap, -1, target)
+        target = (col + my * fine.by + 2 * coarse.lanes) // 2 - coarse.lanes
+        up = (there == target) & ~gap
     else:
-        target = lane_map(fine, coarse, lane)
-    cols = ones_where(iota(shape, 0) == target)
-    shape = (fine.rows, coarse.rows)
-    row = iota(shape, 0)
-    if fine.split and not coarse.split:
-        row = row - fine.halo + mx * fine.bx
-        row = (row + 2 * fine.rows) // 2 - fine.rows
-    else:
-        row = row // 2
-    rows = ones_where(row == iota(shape, 1))
-    return left(rows, right(x, cols))
+        up = there == lane_map(fine, coarse, lane)
+    return ones_where(down), ones_where(up)
 
 
 def block_sum(x, first, count, factor, columns, place, lanes):
@@ -222,7 +238,7 @@
     shape = (x.shape[1], lanes)
     lane = iota(shape, 0)
     cols = ones_where((lane < columns) & (lane // factor + place == iota(shape, 1)))
-    return left(rows, right(x, cols))
+    return right(left(rows, x), cols)
 
 
 def kernel(levels, dx, dy, *refs):
@@ -231,9 +247,11 @@
     held = []
     refs = refs[14:]
     for _ in levels:
-        held.append(refs[:6])
-        refs = refs[6:]
-    load_sem, halo_send, halo_recv, y_send, y_recv, x_send, x_recv = refs
+        held.append(refs[:7])
+        refs = refs[7:]
+    downs, ups = refs[: LEVELS - 1], refs[LEVELS - 1 : 2 * LEVELS - 2]
+    refs = refs[2 * LEVELS - 2 :]
+    stage, out_sem, load_sem, halo_send, halo_recv, y_send, y_recv, x_send, x_recv = refs
 
     mx, my = lax.axis_index("gx"), lax.axis_index("gy")
     top = levels[0]
@@ -264,7 +282,7 @@
     for i in (0, 2):
         ext[i, 0:G, :] = zero
         ext[i, G + top.rows :, :] = zero
-    for level, (a, v, u, k, s, r) in zip(levels, held):
+    for level, (a, v, u, k, s, r, c) in zip(levels, held):
         for ref in (v, u, k):
             ref[0:G, :] = jnp.zeros((G, level.lanes), F32)
             ref[G + level.rows :, :] = jnp.zeros((G, level.lanes), F32)
@@ -352,6 +370,9 @@
         gca[my, i] = scale * block_sum(x, 0, gx_rows, factor, by, place, whole.lanes)
     coef_y = over_gy(gca, 0)
 
+    for depth in range(LEVELS - 1):
+        downs[depth][...], ups[depth][...] = matrices(levels[depth], levels[depth + 1], my)
+
     for copy, _, back in halos:
         pl.when(back)(copy.wait_recv)
 
@@ -376,7 +397,7 @@
             for j in range(4):
                 ext[j, pl.ds(first, HALO), pl.ds(0, by)] = jnp.zeros((HALO, by), F32)
 
-    setup(top, mx, my, ext.at[2], ext.at[3, pl.ds(G, top.rows)], held[0][0], ext.at[1])
+    setup(top, ext.at[2], ext.at[3, pl.ds(G, top.rows)], held[0][0], held[0][6], ext.at[1])
 
     for copy in coef_y:
         copy.wait_recv()
@@ -388,56 +409,67 @@
     def inner(level, ref):
         return ref[pl.ds(G, level.rows), :]
 
+    def coarse_terms(depth):
+        level = levels[depth]
+        a, _, _, k, s, _, pairs = held[depth]
+        fine = held[depth - 1][6]
+        both = jnp.concatenate([pair_rows(fine.at[0]), pair_rows(fine.at[1])], axis=0)
+        both = right(both, downs[depth - 1][...])
+        k[pl.ds(G, level.rows), :] = 0.5 * both[: level.rows]
+        s[...] = both[level.rows :]
+        needed = depth != LOCAL - 1 and depth != LEVELS - 1
+        setup(level, k, s, a, pairs if needed else None)
+
+    def first_sweep(depth, side):
+        level = levels[depth]
+        a, v = held[depth][:2]
+        first = a[5] * side
+        a[4] = first
+        v[pl.ds(G, level.rows), :] = first
+
     for depth in range(LOCAL):
         level = levels[depth]
-        a, v, u, k, s, res = held[depth]
+        a, v, u, k, s, res, _ = held[depth]
         if depth == 0:
             sweep(level, ext.at[0], v, a)
         else:
-            fine = levels[depth - 1]
-            fk, fs = (ext.at[2], ext.at[3, pl.ds(G, top.rows)]) if depth == 1 else held[depth - 1][3:5]
-            k[pl.ds(G, level.rows), :] = 0.5 * coarsen(fine, level, inner(fine, fk))
-            s[...] = coarsen(fine, level, fs[...])
-            setup(level, mx, my, k, s, a)
-            first = a[5] * coarsen(fine, level, held[depth - 1][5][...])
-            a[4] = first
-            v[pl.ds(G, level.rows), :] = first
+            coarse_terms(depth)
+            first_sweep(depth, right(pair_rows(held[depth - 1][5]), downs[depth - 1][...]))
         sweep(level, v, u, a)
         residual(level, u, res, a)
 
     last = levels[LOCAL - 1]
-    ga[my] = block_sum(held[LOCAL - 1][5][...], last.halo, gx_rows, 2, last.by, place, whole.lanes)
+    edge = last.halo // 2
+    side = right(pair_rows(held[LOCAL - 1][5]), downs[LOCAL - 1][...])
+    ga[my] = side[edge : edge + gx_rows]
     side_y = over_gy(ga, dy)
 
     for copy in coef_x:
         copy.wait_recv()
-    for depth in range(LOCAL, LEVELS):
-        level = levels[depth]
-        a, v, u, k, s, res = held[depth]
-        if depth == LOCAL:
-            k[pl.ds(G, level.rows), :] = gcb[0]
-            s[...] = gcb[1]
-        else:
-            fine = levels[depth - 1]
-            k[pl.ds(G, level.rows), :] = 0.5 * coarsen(fine, level, inner(fine, held[depth - 1][3]))
-            s[...] = coarsen(fine, level, held[depth - 1][4][...])
-        setup(level, mx, my, k, s, a)
+    a, _, _, k, s, _, pairs = held[LOCAL]
+    k[pl.ds(G, whole.rows), :] = gcb[0]
+    s[...] = gcb[1]
+    setup(whole, k, s, a, pairs)
 
     for copy in side_y:
         copy.wait_recv()
     part = pl.ds(pl.multiple_of(mx * gx_rows, 8), gx_rows)
     gb[part, :] = functools.reduce(lambda x, y: x + y, [ga[j] for j in range(dy)])
     side_x = over_gx(gb.at[part], dx)
+
+    for depth in range(LOCAL + 1, LEVELS):
+        coarse_terms(depth)
+
     for copy in side_x:
         copy.wait_recv()
 
     for depth in range(LOCAL, LEVELS):
         level = levels[depth]
-        a, v, u, k, s, res = held[depth]
-        side = gb[...] if depth == LOCAL else coarsen(levels[depth - 1], level, held[depth - 1][5][...])
-        first = a[5] * side
-        a[4] = first
-        v[pl.ds(G, level.rows), :] = first
+        a, v, u, k, s, res, _ = held[depth]
+        if depth == LOCAL:
+            first_sweep(depth, gb[...])
+        else:
+            first_sweep(depth, right(pair_rows(held[depth - 1][5]), downs[depth - 1][...]))
         if depth < LEVELS - 1:
             sweep(level, v, u, a)
             residual(level, u, res, a)
@@ -449,8 +481,16 @@
 
     for depth in reversed(range(LEVELS - 1)):
         level, below = levels[depth], levels[depth + 1]
-        a, v, u, k, s, res = held[depth]
-        u[pl.ds(G, level.rows), :] += prolong(level, below, mx, my, inner(below, held[depth + 1][2]))
+        a, v, u, k, s, res, _ = held[depth]
+        error = held[depth + 1][2]
+        if depth == LOCAL - 1:
+            window = error[pl.ds(pl.multiple_of(mx * gx_rows, 8), gx_rows + 2 * G), :]
+            wide = right(window, ups[depth][...])[G - edge : G + gx_rows + edge]
+        else:
+            wide = right(error[pl.ds(G, below.rows), :], ups[depth][...])
+        repeat_rows(res, wide)
+        tiles = [res[t] for t in range(level.lanes // 128)]
+        u[pl.ds(G, level.rows), :] += jnp.concatenate(tiles, axis=1)
         if depth:
             sweep(level, u, v, a)
             sweep(level, v, u, a)
@@ -459,14 +499,22 @@
             sweep(level, u, v, a, HALO - step, bx + 2 * step)
 
             def put(r, rows, mid, new):
-                out_ref[pl.ds(r - HALO, step), :] = new[:, :by]
-
-            smooth(level, v, a, put, HALO, bx)
+                stage[pl.ds(r - HALO, step), :] = new[:, :by]
+
+            half = bx // 2
+            results = []
+            for i in range(2):
+                smooth(level, v, a, put, HALO + i * half, half)
+                part = pl.ds(i * half, half)
+                results.append(pltpu.make_async_copy(stage.at[part], out_ref.at[part], out_sem.at[i]))
+                results[-1].start()
 
     for copy, ok, _ in halos:
         pl.when(ok)(copy.wait_send)
     for copy in sends:
         copy.wait_send()
+    for copy in results:
+        copy.wait()
 
 
 def per_device(nx, ny, pressure, source, conductivity, storage):
@@ -488,7 +536,12 @@
     ]
     for level in levels:
         scratch += level.scratch()
+    pairs = list(zip(levels, levels[1:]))
+    scratch += [pltpu.VMEM((fine.lanes, coarse.lanes), jnp.bfloat16) for fine, coarse in pairs]
+    scratch += [pltpu.VMEM((coarse.lanes, fine.lanes), jnp.bfloat16) for fine, coarse in pairs]
     scratch += [
+        pltpu.VMEM((bx, by), F32),
+        pltpu.SemaphoreType.DMA((2,)),
         pltpu.SemaphoreType.DMA((4,)),
         pltpu.SemaphoreType.DMA((8,)),
         pltpu.SemaphoreType.DMA((8,)),
@@ -501,7 +554,7 @@
         functools.partial(kernel, levels, dx, dy),
         out_shape=jax.ShapeDtypeStruct((bx, by), F32),
         in_specs=[pl.BlockSpec(memory_space=pltpu.HBM)] * 4,
-        out_specs=pl.BlockSpec(memory_space=pltpu.VMEM),
+        out_specs=pl.BlockSpec(memory_space=pltpu.HBM),
         scratch_shapes=scratch,
         compiler_params=pltpu.CompilerParams(
             collective_id=0, has_side_effects=True, vmem_limit_bytes=62 * 2**20

time: 35.5 us -> 33.6 us (0.946)
  Pallas kernels: 33.4 us -> 31.5 us
    pallas_call x1, Pallas kernels: 33.4 us -> 31.5 us  [per_device(): pl.pallas_call(functools.partial(kernel, levels, dx, dy), out_shape=jax.S...]
where the time goes in v3:
time: 33.6 us; the launch traced here: 33.1 us
  Pallas kernels  31.5 us (94%)
  local copies, waits for them, and re-layouts  1.67 us (5%)
    pallas_call x1, Pallas kernels, per_device(): pl.pallas_call(functools.partial(kernel, levels, dx, dy), out_shape=jax.S...  31.5 us
    unnamed x1, local copies, waits for them, and re-layouts  1.67 us

profile of v3, /device:TPU:1, one launch (start us, length us, event | category | flops | bytes accessed | tf_op | source)
XLA Modules:
  0.0 33.1 jit_solution(13575915738167808399)
XLA Ops:
  0.0 31.5 %shard_map.46 = f32[256,256]{1,0:T(8,128)} custom-call(f32[256,256]{1,0:T(8,128)} %refs_0_.1, f32[256,256]{1,0:T(8,128)} %refs_1_.1, f32[256,256]{1,0:T(8,128)} %refs_2_.1, f32[256,256]{1,0:T(8,128)} %refs_3_.1), custom_call_target="tpu_custom_call" | custom-call | tf_op jit(solution)/shard_map/pallas_call | solution.py:553
  31.5 1.7 %copy.6 = f32[256,256]{1,0:T(8,128)} copy(f32[256,256]{1,0:T(8,128)} %shard_map.46) | data formatting | bytes 524288

commit v4 on v3

v4 whole, which is shorter than its diff:
```python
import functools

import jax
import jax.numpy as jnp
from jax import lax
from jax.experimental import pallas as pl
from jax.experimental.pallas import tpu as pltpu
from jax.sharding import PartitionSpec as P

LEVELS_SPLIT = 4
LEVELS_MERGED = 2
COARSE_SWEEPS = 8
OMEGA = 0.8

LOCAL = LEVELS_SPLIT - 1
LEVELS = LEVELS_SPLIT + LEVELS_MERGED
HALOS = (8, 16, 8)
G = 8
MESH = pl.DeviceIdType.MESH
F32 = jnp.float32


def round_up(n, m):
    return -(-n // m) * m


def iota(shape, dim):
    return lax.broadcasted_iota(jnp.int32, shape, dim)


def ones_where(mask):
    return jnp.where(mask, 1.0, 0.0).astype(jnp.bfloat16)


def parts(x):
    high = x.astype(jnp.bfloat16)
    low = (x - high.astype(F32)).astype(jnp.bfloat16)
    return high, low


def dot(a, b):
    return jnp.dot(a, b, preferred_element_type=F32)


def left(matrix, x):
    high, low = parts(x)
    return dot(matrix, high) + dot(matrix, low)


def right(x, matrix):
    high, low = parts(x)
    return dot(high, matrix) + dot(low, matrix)


def put_tiles(ref, rows, x):
    for t in range(x.shape[1] // 128):
        ref[t, rows, :] = x[:, 128 * t : 128 * t + 128]


def pair_rows(ref):
    tiles, rows, _ = ref.shape
    first, second = pl.ds(0, rows // 2, stride=2), pl.ds(1, rows // 2, stride=2)
    return jnp.concatenate([ref[t, first, :] + ref[t, second, :] for t in range(tiles)], axis=1)


def repeat_rows(ref, x):
    tiles, rows, _ = ref.shape
    for t in range(tiles):
        part = x[:, 128 * t : 128 * t + 128]
        ref[t, pl.ds(0, rows // 2, stride=2), :] = part
        ref[t, pl.ds(1, rows // 2, stride=2), :] = part


class Level:
    def __init__(self, depth, bx, by, nx, ny):
        self.depth = depth
        self.split = depth < LOCAL
        self.nx, self.ny = nx >> depth, ny >> depth
        if self.split:
            self.halo = HALOS[depth]
            self.bx, self.by = bx >> depth, by >> depth
            self.rows = self.bx + 2 * self.halo
            self.lanes = round_up(self.by + 2 * self.halo, 128)
        else:
            self.halo = 0
            self.bx, self.by = self.nx, self.ny
            self.rows = self.nx
            self.lanes = round_up(self.ny, 128)
        self.step = 32 if self.lanes > 128 else 128

    def scratch(self):
        tall = pltpu.VMEM((self.rows + 2 * G, self.lanes), F32)
        flat = pltpu.VMEM((self.rows, self.lanes), F32)
        tiled = (self.lanes // 128, self.rows, 128)
        return [
            pltpu.VMEM((7, self.rows, self.lanes), F32), tall, tall, tall, flat,
            pltpu.VMEM(tiled, F32), pltpu.VMEM((2, *tiled), F32),
        ]


def neighbours(win, count, lanes):
    mid = win[G : G + count]
    size = count + 2 * G
    up = pltpu.roll(win, 1, 0)[G : G + count]
    down = pltpu.roll(win, size - 1, 0)[G : G + count]
    before = pltpu.roll(mid, 1, 1)
    after = pltpu.roll(mid, lanes - 1, 1)
    return mid, up, down, before, after


def loop(start, count, step, body):
    for r in range(0, count, step):
        body(start + r, min(step, count - r))


def setup(level, k_ref, s_ref, a_ref, pairs=None, source=None):
    def body(r, count):
        mid, up, down, before, after = neighbours(
            k_ref[pl.ds(r, count + 2 * G), :], count, level.lanes
        )
        inside = mid > 0.0
        if not level.split:
            lane = iota(mid.shape, 1)
            before = jnp.where(lane == 0, 0.0, before)
            after = jnp.where(lane == level.lanes - 1, 0.0, after)
        west, east = 0.5 * (mid + up), 0.5 * (mid + down)
        south, north = 0.5 * (mid + before), 0.5 * (mid + after)
        rows = pl.ds(r, count)
        stored = s_ref[rows, :]
        diag = stored + west + east + south + north
        c = jnp.where(inside, OMEGA / diag, 0.0)
        a_ref[0, rows, :] = c * west
        a_ref[1, rows, :] = c * east
        if level.split:
            a_ref[2, rows, :] = c * south
            a_ref[3, rows, :] = c * north
        else:
            a_ref[2, rows, :] = jnp.where(lane == 0, 0.0, c * south)
            a_ref[3, rows, :] = jnp.where(lane == level.ny - 1, 0.0, c * north)
        a_ref[5, rows, :] = c
        a_ref[6, rows, :] = diag * (1.0 / OMEGA)
        if pairs is not None:
            put_tiles(pairs.at[0], rows, mid)
            put_tiles(pairs.at[1], rows, stored)
        if source is not None:
            a_ref[4, rows, :] = c * source[rows_of(r, count), :]

    loop(0, level.rows, level.step, body)


def rows_of(r, count):
    return pl.ds(r + G, count)


def smooth(level, src, a_ref, put, start=0, total=None):
    def body(r, count):
        mid, up, down, before, after = neighbours(
            src[pl.ds(r, count + 2 * G), :], count, level.lanes
        )
        rows = pl.ds(r, count)
        new = (1.0 - OMEGA) * mid + a_ref[4, rows, :]
        new = new + (a_ref[0, rows, :] * up + a_ref[1, rows, :] * down)
        new = new + (a_ref[2, rows, :] * before + a_ref[3, rows, :] * after)
        put(r, rows, mid, new)

    loop(start, level.rows if total is None else total, level.step, body)


def sweep(level, src, dst, a_ref, start=0, total=None):
    def put(r, rows, mid, new):
        dst[rows_of(r, rows.size), :] = new

    smooth(level, src, a_ref, put, start, total)


def residual(level, src, dst, a_ref):
    def put(r, rows, mid, new):
        put_tiles(dst, rows, (new - mid) * a_ref[6, rows, :])

    smooth(level, src, a_ref, put)


def residual_own(level, src, dst, a_ref):
    def put(r, rows, mid, new):
        part = (new - mid) * a_ref[6, rows, :]
        put_tiles(dst, pl.ds(r - level.halo, rows.size), part[:, : level.by])

    smooth(level, src, a_ref, put, level.halo, level.bx)


def lane_map(fine, coarse, lane):
    half = lane // 2
    if fine.split:
        shift = coarse.lanes - fine.lanes // 2
        half = jnp.where(lane >= fine.lanes - fine.halo, half + shift, half)
    return half


def matrices(fine, coarse, my):
    shape = (fine.by, coarse.by) if fine.depth == 0 else (fine.lanes, coarse.lanes)
    lane, there = iota(shape, 0), iota(shape, 1)
    if fine.depth == 0:
        down = lane // 2 == there
    elif fine.split and not coarse.split:
        down = (lane < fine.by) & (lane // 2 + my * (fine.by // 2) == there)
    else:
        down = lane_map(fine, coarse, lane) == there
    shape = (coarse.lanes, fine.lanes)
    there, lane = iota(shape, 0), iota(shape, 1)
    if fine.split and not coarse.split:
        col = jnp.where(lane >= fine.lanes - fine.halo, lane - fine.lanes, lane)
        gap = (lane >= fine.by + fine.halo) & (lane < fine.lanes - fine.halo)
        target = (col + my * fine.by + 2 * coarse.lanes) // 2 - coarse.lanes
        up = (there == target) & ~gap
    else:
        up = there == lane_map(fine, coarse, lane)
    return ones_where(down), ones_where(up)


def block_sum(x, count, factor, place):
    shape = (count, x.shape[0])
    rows = ones_where(iota(shape, 1) // factor == iota(shape, 0))
    shape = (x.shape[1], 128)
    cols = ones_where(iota(shape, 0) // factor + place == iota(shape, 1))
    return right(left(rows, x), cols)


class Exchange:
    def __init__(self, ext, scratch, level, here, size):
        self.ext, self.level = ext, level
        self.strips, self.halos = scratch[:2], scratch[2:4]
        self.mx, self.my = here
        self.dx, self.dy = size
        self.count, self.width = ext.shape[0], level.halo
        self.groups = 128 // (self.count * self.width)
        self.rows = level.bx // self.groups
        self.copies = []
        bx, by, w, rows = level.bx, level.by, self.width, self.rows
        for n, (sx, sy) in enumerate((i, j) for i in (-1, 0, 1) for j in (-1, 0, 1) if i or j):
            if sy == 0:
                first = G + w if sx < 0 else G + bx
                there = G + w + bx if sx < 0 else G
                src = ext.at[:, pl.ds(first, w), pl.ds(0, by)]
                dst = ext.at[:, pl.ds(there, w), pl.ds(0, by)]
            else:
                mine, theirs = (self.strips[0], self.halos[1]) if sy < 0 else (self.strips[1], self.halos[0])
                if sx == 0:
                    src, dst = mine, theirs.at[pl.ds(w, rows)]
                elif sx < 0:
                    src, dst = mine.at[pl.ds(0, w)], theirs.at[pl.ds(w + rows, w)]
                else:
                    src, dst = mine.at[pl.ds(rows - w, w)], theirs.at[pl.ds(0, w)]
            copy = pltpu.make_async_remote_copy(
                src_ref=src, dst_ref=dst, send_sem=scratch[4].at[n], recv_sem=scratch[5].at[n],
                device_id=(self.mx + sx, self.my + sy), device_id_type=MESH,
            )
            self.copies.append((copy, self.there(sx, sy), self.there(-sx, -sy)))

    @staticmethod
    def scratch(level, count):
        rows = level.bx * level.halo * count // 128
        strip, halo = pltpu.VMEM((rows, 128), F32), pltpu.VMEM((rows + 2 * level.halo, 128), F32)
        return [strip, strip, halo, halo, pltpu.SemaphoreType.DMA((8,)), pltpu.SemaphoreType.DMA((8,))]

    def there(self, sx, sy):
        x, y = self.mx + sx, self.my + sy
        return (x >= 0) & (x < self.dx) & (y >= 0) & (y < self.dy)

    def pack(self):
        level, w = self.level, self.width
        slot = iota((self.rows, 128), 1) // w
        for strip, first, at in ((self.strips[0], 0, 0), (self.strips[1], level.by - 128, 128 - w)):
            packed = None
            for i in range(self.count * self.groups):
                group, j = divmod(i, self.count)
                x = self.ext[j, pl.ds(G + w + group * self.rows, self.rows), pl.ds(first, 128)]
                turn = (w * i - at) % 128
                if turn:
                    x = pltpu.roll(x, turn, 1)
                packed = x if packed is None else jnp.where(slot == i, x, packed)
            strip[...] = packed

    def start(self):
        for copy, ok, _ in self.copies:
            pl.when(ok)(copy.start)

    def finish(self):
        for copy, _, back in self.copies:
            pl.when(back)(copy.wait_recv)
        level, w, rows = self.level, self.width, self.rows
        tile = pl.ds(level.lanes - 128, 128)
        blocks = [(0, w, self.groups - 1, G), (w + rows, w, 0, G + w + level.bx)]
        blocks += [(w, rows, g, G + w + g * rows) for g in range(self.groups)]
        for first, count, group, there in blocks:
            lower, upper = (ref[pl.ds(first, count), :] for ref in self.halos)
            lane = iota((count, 128), 1)
            right_part = (lane < w) & (self.my < self.dy - 1)
            left_part = (lane >= 128 - w) & (self.my > 0)
            for j in range(self.count):
                at = (group * self.count + j) * w
                turn_l, turn_r = (128 - w - at) % 128, -at % 128
                x = pltpu.roll(lower, turn_l, 1) if turn_l else lower
                y = pltpu.roll(upper, turn_r, 1) if turn_r else upper
                x = jnp.where(right_part, y, jnp.where(left_part, x, 0.0))
                self.ext[j, pl.ds(there, count), tile] = x
        for edge, first in ((self.mx == 0, G), (self.mx == self.dx - 1, G + w + level.bx)):
            @pl.when(edge)
            def _():
                self.ext[:, pl.ds(first, w), :] = jnp.zeros((self.count, w, level.lanes), F32)

    def drain(self):
        for copy, ok, _ in self.copies:
            pl.when(ok)(copy.wait_send)


def kernel(levels, dx, dy, *refs):
    p_hbm, s_hbm, k_hbm, st_hbm, out_ref = refs[:5]
    ext, ext_coef, ext_side, own_res, own_pairs, ga, gb, gca, gcb = refs[5:14]
    refs = refs[14:]
    ex_scratch, refs = [refs[:6], refs[6:12], refs[12:18]], refs[18:]
    held = []
    for _ in levels:
        held.append(list(refs[:7]))
        refs = refs[7:]
    downs, ups = refs[: LEVELS - 1], refs[LEVELS - 1 : 2 * LEVELS - 2]
    refs = refs[2 * LEVELS - 2 :]
    stage, out_sem, load_sem, y_send, y_recv, x_send, x_recv = refs

    mx, my = lax.axis_index("gx"), lax.axis_index("gy")
    top, second = levels[:2]
    bx, by = top.bx, top.by
    own = pl.ds(G + top.halo, bx)
    held[1][3], held[1][4] = ext_coef.at[0], ext_coef.at[1, pl.ds(G, second.rows)]

    loads, tiled_loads = [], []
    for i, ref in enumerate((p_hbm, s_hbm, k_hbm, st_hbm)):
        loads.append(pltpu.make_async_copy(ref, ext.at[i, own, pl.ds(0, by)], load_sem.at[i]))
        loads[-1].start()
    for i, ref in enumerate((k_hbm, st_hbm)):
        for t in range(by // 128):
            tiled_loads.append(pltpu.make_async_copy(
                ref.at[:, pl.ds(128 * t, 128)], own_pairs.at[i, t], load_sem.at[4 + i * (by // 128) + t]
            ))
            tiled_loads[-1].start()

    halo = Exchange(ext, ex_scratch[0], top, (mx, my), (dx, dy))
    halo_coef = Exchange(ext_coef, ex_scratch[1], second, (mx, my), (dx, dy))
    halo_side = Exchange(ext_side, ex_scratch[2], second, (mx, my), (dx, dy))

    barrier = pltpu.get_barrier_semaphore()
    for d in range(1, dx):
        pl.semaphore_signal(barrier, inc=1, device_id=(lax.rem(mx + d, dx), my), device_id_type=MESH)
    for d in range(1, dy):
        pl.semaphore_signal(barrier, inc=1, device_id=(mx, lax.rem(my + d, dy)), device_id_type=MESH)
    signals = dx - 1 + dy - 1
    for sx in (-1, 1):
        for sy in (-1, 1):
            ok = halo.there(sx, sy)
            signals = signals + jnp.where(ok, 1, 0)
            @pl.when(ok)
            def _():
                pl.semaphore_signal(barrier, inc=1, device_id=(mx + sx, my + sy), device_id_type=MESH)

    for ref, level in ((ext.at[0], top), (ext.at[2], top), (ext_coef.at[0], second)):
        ref[0:G, :] = jnp.zeros((G, level.lanes), F32)
        ref[G + level.rows :, :] = jnp.zeros((G, level.lanes), F32)
    for level, (a, v, u, k, s, r, c) in zip(levels, held):
        for ref in (v, u, k):
            ref[0:G, :] = jnp.zeros((G, level.lanes), F32)
            ref[G + level.rows :, :] = jnp.zeros((G, level.lanes), F32)
    downs[0][...], ups[0][...] = matrices(top, second, my)

    for copy in loads:
        copy.wait()
    halo.pack()
    pl.semaphore_wait(barrier, signals)
    halo.start()

    for copy in tiled_loads:
        copy.wait()
    half = bx // 2
    own_second = pl.ds(G + second.halo, half)
    both = jnp.concatenate([pair_rows(own_pairs.at[0]), pair_rows(own_pairs.at[1])], axis=0)
    both = right(both, downs[0][...])
    near_k, near_s = 0.5 * both[:half], both[half:]
    ext_coef[0, own_second, 0 : by // 2] = near_k
    ext_coef[1, own_second, 0 : by // 2] = near_s

    whole = levels[LOCAL]
    factor = 1 << LOCAL
    gx_rows, gy_cols = bx // factor, by // factor
    sends = []

    def send(src, dst, sems, n, target):
        copy = pltpu.make_async_remote_copy(
            src_ref=src, dst_ref=dst, send_sem=sems[0].at[n], recv_sem=sems[1].at[n],
            device_id=target, device_id_type=MESH,
        )
        copy.start()
        sends.append(copy)
        return copy

    def over_gy(buffer, base):
        return [
            send(buffer.at[my], buffer.at[my], (y_send, y_recv), base + d, (mx, lax.rem(my + d, dy)))
            for d in range(1, dy)
        ]

    def strip_of(row):
        return pl.ds(pl.multiple_of(row * gx_rows, 8), gx_rows)

    far_k = 0.5 ** (LOCAL - 1) * block_sum(near_k, gx_rows, factor // 2, 0)
    gca[my] = far_k + block_sum(near_s, gx_rows, factor // 2, gy_cols)
    coef_y = over_gy(gca, 0)
    halo_coef.pack()
    halo_coef.start()

    for depth in range(1, LEVELS - 1):
        downs[depth][...], ups[depth][...] = matrices(levels[depth], levels[depth + 1], my)

    halo.finish()
    setup(top, ext.at[2], ext.at[3, pl.ds(G, top.rows)], held[0][0], None, ext.at[1])

    for copy in coef_y:
        copy.wait_recv()
    lane = iota((gx_rows, whole.lanes), 1)
    for i in range(2):
        merged = jnp.zeros((gx_rows, whole.lanes), F32)
        for j in range(dy):
            first = gy_cols * j
            x = jnp.concatenate([gca[j]] * (whole.lanes // 128), axis=1)
            turn = (first - gy_cols * i) % whole.lanes
            x = pltpu.roll(x, turn, 1) if turn else x
            merged = jnp.where((lane >= first) & (lane < first + gy_cols), x, merged)
        gcb[i, strip_of(mx), :] = merged
    mine = gcb.at[:, strip_of(mx)]
    coef_x = [
        send(mine, mine, (x_send, x_recv), d, (lax.rem(mx + d, dx), my)) for d in range(2, dx, 2)
    ]

    def coarse_terms(depth):
        level = levels[depth]
        a, _, _, k, s, _, pairs = held[depth]
        fine = held[depth - 1][6]
        both = jnp.concatenate([pair_rows(fine.at[0]), pair_rows(fine.at[1])], axis=0)
        both = right(both, downs[depth - 1][...])
        k[pl.ds(G, level.rows), :] = 0.5 * both[: level.rows]
        s[...] = both[level.rows :]
        needed = depth != LOCAL - 1 and depth != LEVELS - 1
        setup(level, k, s, a, pairs if needed else None)

    def first_sweep(depth, side):
        level = levels[depth]
        a, v = held[depth][:2]
        first = a[5] * side
        a[4] = first
        v[pl.ds(G, level.rows), :] = first

    sweep(top, ext.at[0], held[0][1], held[0][0])
    sweep(top, held[0][1], held[0][2], held[0][0])
    residual_own(top, held[0][2], own_res, held[0][0])
    ext_side[0, own_second, 0 : by // 2] = right(pair_rows(own_res), downs[0][...])
    halo_side.pack()
    halo_side.start()

    halo_coef.finish()
    setup(second, held[1][3], held[1][4], held[1][0], held[1][6])
    for depth in range(2, LOCAL):
        coarse_terms(depth)
    for copy in coef_x:
        copy.wait_recv()
    core = lax.rem(mx, 2)
    coef_x = []
    for chip in range(dx // 2):
        part = gcb.at[:, strip_of(2 * chip + core)]
        coef_x.append(send(part, part, (x_send, x_recv), 2 * dx + chip, (mx + 1 - 2 * core, my)))

    halo_side.finish()
    for depth in range(1, LOCAL):
        level = levels[depth]
        a, v, u, k, s, res, _ = held[depth]
        if depth == 1:
            first_sweep(depth, ext_side[0, pl.ds(G, level.rows), :])
        else:
            first_sweep(depth, right(pair_rows(held[depth - 1][5]), downs[depth - 1][...]))
        sweep(level, v, u, a)
        residual(level, u, res, a)

    last = levels[LOCAL - 1]
    edge = last.halo // 2
    side = right(pair_rows(held[LOCAL - 1][5]), downs[LOCAL - 1][...])
    ga[my] = side[edge : edge + gx_rows]
    side_y = over_gy(ga, dy)

    for copy in coef_x:
        copy.wait_recv()
    a, _, _, k, s, _, pairs = held[LOCAL]
    k[pl.ds(G, whole.rows), :] = gcb[0]
    s[...] = gcb[1]
    setup(whole, k, s, a, pairs)

    for copy in side_y:
        copy.wait_recv()
    gb[strip_of(mx), :] = functools.reduce(lambda x, y: x + y, [ga[j] for j in range(dy)])
    mine = gb.at[strip_of(mx)]
    side_x = [
        send(mine, mine, (x_send, x_recv), dx + d, (lax.rem(mx + d, dx), my)) for d in range(1, dx)
    ]

    for depth in range(LOCAL + 1, LEVELS):
        coarse_terms(depth)

    for copy in side_x:
        copy.wait_recv()

    for depth in range(LOCAL, LEVELS):
        level = levels[depth]
        a, v, u, k, s, res, _ = held[depth]
        if depth == LOCAL:
            first_sweep(depth, gb[...])
        else:
            first_sweep(depth, right(pair_rows(held[depth - 1][5]), downs[depth - 1][...]))
        if depth < LEVELS - 1:
            sweep(level, v, u, a)
            residual(level, u, res, a)
        else:
            for i in range(COARSE_SWEEPS - 1):
                sweep(level, *((v, u) if i % 2 == 0 else (u, v)), a)
            if COARSE_SWEEPS % 2:
                u[...] = v[...]

    for depth in reversed(range(LEVELS - 1)):
        level, below = levels[depth], levels[depth + 1]
        a, v, u, k, s, res, _ = held[depth]
        error = held[depth + 1][2]
        if depth == LOCAL - 1:
            window = error[pl.ds(pl.multiple_of(mx * gx_rows, 8), gx_rows + 2 * G), :]
            wide = right(window, ups[depth][...])[G - edge : G + gx_rows + edge]
        else:
            skip = below.halo - level.halo // 2
            wide = right(error[pl.ds(G + skip, below.rows - 2 * skip), :], ups[depth][...])
        repeat_rows(res, wide)
        tiles = [res[t] for t in range(level.lanes // 128)]
        u[pl.ds(G, level.rows), :] += jnp.concatenate(tiles, axis=1)
        if depth:
            sweep(level, u, v, a)
            sweep(level, v, u, a)
        else:
            sweep(level, u, v, a)

            def put(r, rows, mid, new):
                stage[pl.ds(r - level.halo, rows.size), :] = new[:, :by]

            half = bx // 2
            results = []
            for i in range(2):
                smooth(level, v, a, put, level.halo + i * half, half)
                part = pl.ds(i * half, half)
                results.append(pltpu.make_async_copy(stage.at[part], out_ref.at[part], out_sem.at[i]))
                results[-1].start()

    for exchange in (halo, halo_coef, halo_side):
        exchange.drain()
    for copy in sends:
        copy.wait_send()
    for copy in results:
        copy.wait()


def per_device(nx, ny, pressure, source, conductivity, storage):
    dx, dy = lax.axis_size("gx"), lax.axis_size("gy")
    bx, by = pressure.shape
    levels = [Level(depth, bx, by, nx, ny) for depth in range(LEVELS)]
    top, second, whole = levels[0], levels[1], levels[LOCAL]
    rows, tiles = bx >> LOCAL, by // 128
    scratch = [
        pltpu.VMEM((4, top.rows + 2 * G, top.lanes), F32),
        pltpu.VMEM((2, second.rows + 2 * G, second.lanes), F32),
        pltpu.VMEM((1, second.rows + 2 * G, second.lanes), F32),
        pltpu.VMEM((tiles, bx, 128), F32),
        pltpu.VMEM((2, tiles, bx, 128), F32),
        pltpu.VMEM((dy, rows, whole.lanes), F32),
        pltpu.VMEM((whole.rows, whole.lanes), F32),
        pltpu.VMEM((dy, rows, 128), F32),
        pltpu.VMEM((2, whole.rows, whole.lanes), F32),
    ]
    for level, count in ((top, 4), (second, 2), (second, 1)):
        scratch += Exchange.scratch(level, count)
    for level in levels:
        scratch += level.scratch()
    pairs = list(zip(levels, levels[1:]))
    scratch += [
        pltpu.VMEM((fine.lanes, coarse.lanes) if fine.depth else (by, by // 2), jnp.bfloat16)
        for fine, coarse in pairs
    ]
    scratch += [pltpu.VMEM((coarse.lanes, fine.lanes), jnp.bfloat16) for fine, coarse in pairs]
    scratch += [
        pltpu.VMEM((bx, by), F32),
        pltpu.SemaphoreType.DMA((2,)),
        pltpu.SemaphoreType.DMA((4 + 2 * tiles,)),
        pltpu.SemaphoreType.DMA((2 * dy,)),
        pltpu.SemaphoreType.DMA((2 * dy,)),
        pltpu.SemaphoreType.DMA((3 * dx,)),
        pltpu.SemaphoreType.DMA((3 * dx,)),
    ]
    return pl.pallas_call(
        functools.partial(kernel, levels, dx, dy),
        out_shape=jax.ShapeDtypeStruct((bx, by), F32),
        in_specs=[pl.BlockSpec(memory_space=pltpu.HBM)] * 4,
        out_specs=pl.BlockSpec(memory_space=pltpu.HBM),
        scratch_shapes=scratch,
        compiler_params=pltpu.CompilerParams(
            collective_id=0, has_side_effects=True, vmem_limit_bytes=62 * 2**20
        ),
    )(pressure, source, conductivity, storage)


def solution(mesh):
    placed = (P("gx", "gy"), P("gx", "gy"), P("gx", "gy"), P("gx", "gy"))

    def run(pressure, source, conductivity, storage):
        nx, ny = pressure.shape
        return jax.shard_map(
            functools.partial(per_device, nx, ny),
            mesh=mesh, in_specs=placed, out_specs=P("gx", "gy"), check_vma=False,
        )(pressure, source, conductivity, storage)

    return run
```

time: 33.6 us -> 30.7 us (0.914)
  Pallas kernels: 31.5 us -> 28.8 us
    pallas_call x1, Pallas kernels: 31.5 us -> 28.8 us  [per_device(): pl.pallas_call(functools.partial(kernel, levels, dx, dy), out_shape=jax.S...]
where the time goes in v4:
time: 30.7 us; the launch traced here: 30.5 us
  Pallas kernels  28.8 us (94%)
  local copies, waits for them, and re-layouts  1.67 us (5%)
    pallas_call x1, Pallas kernels, per_device(): pl.pallas_call(functools.partial(kernel, levels, dx, dy), out_shape=jax.S...  28.8 us
    unnamed x1, local copies, waits for them, and re-layouts  1.67 us

profile of v4, /device:TPU:1, one launch (start us, length us, event | category | flops | bytes accessed | tf_op | source)
XLA Modules:
  0.0 30.5 jit_solution(7838711834229129311)
XLA Ops:
  0.0 28.8 %shard_map.46 = f32[256,256]{1,0:T(8,128)} custom-call(f32[256,256]{1,0:T(8,128)} %refs_0_.1, f32[256,256]{1,0:T(8,128)} %refs_1_.1, f32[256,256]{1,0:T(8,128)} %refs_2_.1, f32[256,256]{1,0:T(8,128)} %refs_3_.1), custom_call_target="tpu_custom_call" | custom-call | tf_op jit(solution)/shard_map/pallas_call | solution.py:606
  28.9 1.7 %copy.6 = f32[256,256]{1,0:T(8,128)} copy(f32[256,256]{1,0:T(8,128)} %shard_map.46) | data formatting | bytes 524288

commit v5 on v4

--- a/solution.py
+++ b/solution.py
@@ -202,7 +202,7 @@
     if fine.depth == 0:
         down = lane // 2 == there
     elif fine.split and not coarse.split:
-        down = (lane < fine.by) & (lane // 2 + my * (fine.by // 2) == there)
+        down = (lane < fine.by) & (lane // 2 == there)
     else:
         down = lane_map(fine, coarse, lane) == there
     shape = (coarse.lanes, fine.lanes)
@@ -368,7 +368,7 @@
         for ref in (v, u, k):
             ref[0:G, :] = jnp.zeros((G, level.lanes), F32)
             ref[G + level.rows :, :] = jnp.zeros((G, level.lanes), F32)
-    downs[0][...], ups[0][...] = matrices(top, second, my)
+    downs[0][...] = matrices(top, second, my)[0]
 
     for copy in loads:
         copy.wait()
@@ -415,24 +415,29 @@
     halo_coef.pack()
     halo_coef.start()
 
-    for depth in range(1, LEVELS - 1):
-        downs[depth][...], ups[depth][...] = matrices(levels[depth], levels[depth + 1], my)
+    for depth in range(1, LOCAL):
+        downs[depth][...] = matrices(levels[depth], levels[depth + 1], my)[0]
 
     halo.finish()
     setup(top, ext.at[2], ext.at[3, pl.ds(G, top.rows)], held[0][0], None, ext.at[1])
 
     for copy in coef_y:
         copy.wait_recv()
-    lane = iota((gx_rows, whole.lanes), 1)
-    for i in range(2):
-        merged = jnp.zeros((gx_rows, whole.lanes), F32)
+
+    def merge(ref, i):
+        shape = (ref.shape[1], whole.lanes)
+        lane = iota(shape, 1)
+        merged = jnp.zeros(shape, F32)
         for j in range(dy):
             first = gy_cols * j
-            x = jnp.concatenate([gca[j]] * (whole.lanes // 128), axis=1)
+            x = jnp.concatenate([ref[j]] * (whole.lanes // 128), axis=1)
             turn = (first - gy_cols * i) % whole.lanes
             x = pltpu.roll(x, turn, 1) if turn else x
             merged = jnp.where((lane >= first) & (lane < first + gy_cols), x, merged)
-        gcb[i, strip_of(mx), :] = merged
+        return merged
+
+    for i in range(2):
+        gcb[i, strip_of(mx), :] = merge(gca, i)
     mine = gcb.at[:, strip_of(mx)]
     coef_x = [
         send(mine, mine, (x_send, x_recv), d, (lax.rem(mx + d, dx), my)) for d in range(2, dx, 2)
@@ -489,7 +494,12 @@
     last = levels[LOCAL - 1]
     edge = last.halo // 2
     side = right(pair_rows(held[LOCAL - 1][5]), downs[LOCAL - 1][...])
-    ga[my] = side[edge : edge + gx_rows]
+    packed = 128 // gy_cols
+    count = gx_rows // packed
+    strip = side[edge : edge + count, :128]
+    for g in range(1, packed):
+        strip = strip + pltpu.roll(side[edge + g * count : edge + (g + 1) * count, :128], g * gy_cols, 1)
+    ga[my] = strip
     side_y = over_gy(ga, dy)
 
     for copy in coef_x:
@@ -501,12 +511,17 @@
 
     for copy in side_y:
         copy.wait_recv()
-    gb[strip_of(mx), :] = functools.reduce(lambda x, y: x + y, [ga[j] for j in range(dy)])
+    for g in range(packed):
+        gb[pl.ds(pl.multiple_of(mx * gx_rows + g * count, 8), count), :] = merge(ga, g)
     mine = gb.at[strip_of(mx)]
     side_x = [
         send(mine, mine, (x_send, x_recv), dx + d, (lax.rem(mx + d, dx), my)) for d in range(1, dx)
     ]
 
+    for depth in range(LEVELS - 1):
+        down, ups[depth][...] = matrices(levels[depth], levels[depth + 1], my)
+        if depth >= LOCAL:
+            downs[depth][...] = down
     for depth in range(LOCAL + 1, LEVELS):
         coarse_terms(depth)
 
@@ -549,7 +564,7 @@
             sweep(level, u, v, a)
 
             def put(r, rows, mid, new):
-                stage[pl.ds(r - level.halo, rows.size), :] = new[:, :by]
+                stage[pl.ds(r - level.halo, rows.size), :] = (1.0 / OMEGA) * new[:, :by]
 
             half = bx // 2
             results = []
@@ -579,7 +594,7 @@
         pltpu.VMEM((1, second.rows + 2 * G, second.lanes), F32),
         pltpu.VMEM((tiles, bx, 128), F32),
         pltpu.VMEM((2, tiles, bx, 128), F32),
-        pltpu.VMEM((dy, rows, whole.lanes), F32),
+        pltpu.VMEM((dy, rows * (by >> LOCAL) // 128, 128), F32),
         pltpu.VMEM((whole.rows, whole.lanes), F32),
         pltpu.VMEM((dy, rows, 128), F32),
         pltpu.VMEM((2, whole.rows, whole.lanes), F32),
@@ -603,7 +618,7 @@
         pltpu.SemaphoreType.DMA((3 * dx,)),
         pltpu.SemaphoreType.DMA((3 * dx,)),
     ]
-    return pl.pallas_call(
+    result = pl.pallas_call(
         functools.partial(kernel, levels, dx, dy),
         out_shape=jax.ShapeDtypeStruct((bx, by), F32),
         in_specs=[pl.BlockSpec(memory_space=pltpu.HBM)] * 4,
@@ -613,6 +628,7 @@
             collective_id=0, has_side_effects=True, vmem_limit_bytes=62 * 2**20
         ),
     )(pressure, source, conductivity, storage)
+    return OMEGA * result
 
 
 def solution(mesh):

time: 30.7 us -> 31.2 us (1.016)
  other arithmetic: 0 us -> 1.68 us
  local copies, waits for them, and re-layouts: 1.67 us -> 0 us
    mul x0 -> x1, other arithmetic: none -> 1.68 us  [per_device(): return OMEGA * result]
    unnamed x1 -> x0, local copies, waits for them, and re-layouts: 1.67 us -> none
where the time goes in v5:
time: 31.2 us; the launch traced here: 30.7 us
  Pallas kernels  29.1 us (93%)
  other arithmetic  1.68 us (5%)
    pallas_call x1, Pallas kernels, per_device(): pl.pallas_call(functools.partial(kernel, levels, dx, dy), out_shape=jax.S...  29.1 us
    mul x1, other arithmetic, per_device(): return OMEGA * result  1.68 us

profile of v5, /device:TPU:1, one launch (start us, length us, event | category | flops | bytes accessed | tf_op | source)
XLA Modules:
  0.0 30.7 jit_solution(5588213091954919124)
XLA Ops:
  0.0 29.1 %shard_map.46 = f32[256,256]{1,0:T(8,128)} custom-call(f32[256,256]{1,0:T(8,128)} %refs_0_.1, f32[256,256]{1,0:T(8,128)} %refs_1_.1, f32[256,256]{1,0:T(8,128)} %refs_2_.1, f32[256,256]{1,0:T(8,128)} %refs_3_.1), custom_call_target="tpu_custom_call" | custom-call | tf_op jit(solution)/shard_map/pallas_call | solution.py:621
  29.1 1.7 %broadcast_multiply_fusion = f32[256,256]{1,0:T(8,128)} fusion(f32[256,256]{1,0:T(8,128)} %shard_map.46), kind=kLoop, calls=%fused_computation | loop fusion | flops 65536 | bytes 524288 | tf_op jit(solution)/shard_map/mul | solution.py:631

commit v6 on v5

--- a/solution.py
+++ b/solution.py
@@ -324,7 +324,7 @@
         refs = refs[7:]
     downs, ups = refs[: LEVELS - 1], refs[LEVELS - 1 : 2 * LEVELS - 2]
     refs = refs[2 * LEVELS - 2 :]
-    stage, out_sem, load_sem, y_send, y_recv, x_send, x_recv = refs
+    load_sem, y_send, y_recv, x_send, x_recv = refs
 
     mx, my = lax.axis_index("gx"), lax.axis_index("gy")
     top, second = levels[:2]
@@ -564,22 +564,14 @@
             sweep(level, u, v, a)
 
             def put(r, rows, mid, new):
-                stage[pl.ds(r - level.halo, rows.size), :] = (1.0 / OMEGA) * new[:, :by]
-
-            half = bx // 2
-            results = []
-            for i in range(2):
-                smooth(level, v, a, put, level.halo + i * half, half)
-                part = pl.ds(i * half, half)
-                results.append(pltpu.make_async_copy(stage.at[part], out_ref.at[part], out_sem.at[i]))
-                results[-1].start()
+                out_ref[pl.ds(r - level.halo, rows.size), :] = new[:, :by]
+
+            smooth(level, v, a, put, level.halo, bx)
 
     for exchange in (halo, halo_coef, halo_side):
         exchange.drain()
     for copy in sends:
         copy.wait_send()
-    for copy in results:
-        copy.wait()
 
 
 def per_device(nx, ny, pressure, source, conductivity, storage):
@@ -610,8 +602,6 @@
     ]
     scratch += [pltpu.VMEM((coarse.lanes, fine.lanes), jnp.bfloat16) for fine, coarse in pairs]
     scratch += [
-        pltpu.VMEM((bx, by), F32),
-        pltpu.SemaphoreType.DMA((2,)),
         pltpu.SemaphoreType.DMA((4 + 2 * tiles,)),
         pltpu.SemaphoreType.DMA((2 * dy,)),
         pltpu.SemaphoreType.DMA((2 * dy,)),
@@ -622,13 +612,13 @@
         functools.partial(kernel, levels, dx, dy),
         out_shape=jax.ShapeDtypeStruct((bx, by), F32),
         in_specs=[pl.BlockSpec(memory_space=pltpu.HBM)] * 4,
-        out_specs=pl.BlockSpec(memory_space=pltpu.HBM),
+        out_specs=pl.BlockSpec(memory_space=pltpu.VMEM),
         scratch_shapes=scratch,
         compiler_params=pltpu.CompilerParams(
-            collective_id=0, has_side_effects=True, vmem_limit_bytes=62 * 2**20
+            collective_id=0, has_side_effects=True, vmem_limit_bytes=428 * 2**17
         ),
     )(pressure, source, conductivity, storage)
-    return OMEGA * result
+    return result
 
 
 def solution(mesh):

time: 31.2 us -> 29.6 us (0.949)
  other arithmetic: 1.68 us -> 0 us
  local copies, waits for them, and re-layouts: 0 us -> 0.71 us
  Pallas kernels: 29.1 us -> 28.4 us
    mul x1 -> x0, other arithmetic: 1.68 us -> none  [per_device(): return OMEGA * result]
    unnamed x0 -> x1, local copies, waits for them, and re-layouts: none -> 0.71 us
    pallas_call x1, Pallas kernels: 29.1 us -> 28.4 us  [per_device(): pl.pallas_call(functools.partial(kernel, levels, dx, dy), out_shape=jax.S...]
where the time goes in v6:
time: 29.6 us; the launch traced here: 29.2 us
  Pallas kernels  28.4 us (96%)
  local copies, waits for them, and re-layouts  0.71 us (2%)
    pallas_call x1, Pallas kernels, per_device(): pl.pallas_call(functools.partial(kernel, levels, dx, dy), out_shape=jax.S...  28.4 us
    unnamed x1, local copies, waits for them, and re-layouts  0.71 us

profile of v6, /device:TPU:1, one launch (start us, length us, event | category | flops | bytes accessed | tf_op | source)
XLA Modules:
  0.0 29.2 jit_solution(13726420329278540228)
XLA Ops:
  0.0 28.4 %shard_map.46 = f32[256,256]{1,0:T(8,128)S(1)} custom-call(f32[256,256]{1,0:T(8,128)} %refs_0_.1, f32[256,256]{1,0:T(8,128)} %refs_1_.1, f32[256,256]{1,0:T(8,128)} %refs_2_.1, f32[256,256]{1,0:T(8,128)} %refs_3_.1), custom_call_target="tpu_custom_call" | custom-call | tf_op jit(solution)/shard_map/pallas_call | solution.py:611
  28.5 0.7 %copy.6 = f32[256,256]{1,0:T(8,128)} copy(f32[256,256]{1,0:T(8,128)S(1)} %shard_map.46) | data formatting | bytes 524288

commit v7 on v6

--- a/solution.py
+++ b/solution.py
@@ -515,8 +515,10 @@
         gb[pl.ds(pl.multiple_of(mx * gx_rows + g * count, 8), count), :] = merge(ga, g)
     mine = gb.at[strip_of(mx)]
     side_x = [
-        send(mine, mine, (x_send, x_recv), dx + d, (lax.rem(mx + d, dx), my)) for d in range(1, dx)
+        send(mine, mine, (x_send, x_recv), dx + d, (lax.rem(mx + d, dx), my)) for d in range(2, dx, 2)
     ]
+    mate = (mx + 1 - 2 * core, my)
+    relayed = [send(mine, mine, (x_send, x_recv), 3 * dx, mate)]
 
     for depth in range(LEVELS - 1):
         down, ups[depth][...] = matrices(levels[depth], levels[depth + 1], my)
@@ -525,7 +527,11 @@
     for depth in range(LOCAL + 1, LEVELS):
         coarse_terms(depth)
 
-    for copy in side_x:
+    for d, copy in zip(range(2, dx, 2), side_x):
+        copy.wait_recv()
+        part = gb.at[strip_of(lax.rem(mx - d + dx, dx))]
+        relayed.append(send(part, part, (x_send, x_recv), 3 * dx + d, mate))
+    for copy in relayed:
         copy.wait_recv()
 
     for depth in range(LOCAL, LEVELS):
@@ -605,8 +611,8 @@
         pltpu.SemaphoreType.DMA((4 + 2 * tiles,)),
         pltpu.SemaphoreType.DMA((2 * dy,)),
         pltpu.SemaphoreType.DMA((2 * dy,)),
-        pltpu.SemaphoreType.DMA((3 * dx,)),
-        pltpu.SemaphoreType.DMA((3 * dx,)),
+        pltpu.SemaphoreType.DMA((4 * dx,)),
+        pltpu.SemaphoreType.DMA((4 * dx,)),
     ]
     result = pl.pallas_call(
         functools.partial(kernel, levels, dx, dy),

time: 29.6 us -> 30.1 us (1.017); the launches traced: 29.2 us -> 30 us
  Pallas kernels: 28.4 us -> 29.3 us
    pallas_call x1, Pallas kernels: 28.4 us -> 29.3 us  [per_device(): pl.pallas_call(functools.partial(kernel, levels, dx, dy), out_shape=jax.S...]
where the time goes in v7:
time: 30.1 us; the launch traced here: 30 us
  Pallas kernels  29.3 us (97%)
  local copies, waits for them, and re-layouts  0.71 us (2%)
    pallas_call x1, Pallas kernels, per_device(): pl.pallas_call(functools.partial(kernel, levels, dx, dy), out_shape=jax.S...  29.3 us
    unnamed x1, local copies, waits for them, and re-layouts  0.71 us

profile of v7, /device:TPU:1, one launch (start us, length us, event | category | flops | bytes accessed | tf_op | source)
XLA Modules:
  0.0 30.0 jit_solution(1065295456755634612)
XLA Ops:
  0.0 29.3 %shard_map.46 = f32[256,256]{1,0:T(8,128)S(1)} custom-call(f32[256,256]{1,0:T(8,128)} %refs_0_.1, f32[256,256]{1,0:T(8,128)} %refs_1_.1, f32[256,256]{1,0:T(8,128)} %refs_2_.1, f32[256,256]{1,0:T(8,128)} %refs_3_.1), custom_call_target="tpu_custom_call" | custom-call | tf_op jit(solution)/shard_map/pallas_call | solution.py:617
  29.3 0.7 %copy.6 = f32[256,256]{1,0:T(8,128)} copy(f32[256,256]{1,0:T(8,128)S(1)} %shard_map.46) | data formatting | bytes 524288
